TPU v7x, 512 devices: a whole 4x4x16 slice. The times are simulated.
512 devices in a mesh: dp: 16 (over z_hi, x, core), seq: 32 (over y, z_lo).
Axes of the slice: x: 4, y: 4, z: 16 (z_hi: 2, z_lo: 8; z = z_hi * 8 + z_lo), core: 2. Of those that a mesh axis runs over, the one named last changes fastest.
Arguments:
- frames: bfloat16 [16, 8192, 1536], P('dp', 'seq'), may hold values from -6 to 6
- lengths: int32 [16], P('dp'), may hold values from 1 to 8192, 38912 in all
- owner_map: int32 [16, 64], P('dp'), may hold values from 0 to 31, as said below
- norm_gain: float32 [1536], replicated, may hold values from 0.5 to 1.5
- norm_bias: float32 [1536], replicated, may hold values from -3 to 3
- proj_weight: bfloat16 [1536, 3072], P('dp'), may hold values from -0.15625 to 0.15625
- dw_kernel: float32 [31, 1536], replicated, may hold values from -1 to 1
- out_grad: bfloat16 [16, 8192, 1536], P('dp', 'seq'), may hold values from -6 to 6
Outputs:
- activations: bfloat16 [16, 8192, 1536], P('dp', 'seq')
- input_grad: bfloat16 [16, 8192, 1536], P('dp', 'seq')
- kernel_grad: float32 [31, 1536], replicated
- gain_grad: float32 [1536], replicated
- bias_grad: float32 [1536], replicated
Inputs may be any that keep to these rules, and one draw needn't show every extreme that they name: The longest utterance has exactly 8192 frames; stored rows from lengths[u] on are padding. owner_map[u, g] = (g + owner_map[u, 0]) mod (32): blocks are dealt in turn to the indices of seq from a starting index drawn per utterance, block g in slot g // 32 of its holder.
All inputs are finite; a program needn't handle non-finite values. No bound on the sum of `lengths` on one device may be relied on, other than what follows from the above.
Results may differ from a plain program's by a relative error of at most 0.0064.
Values may be sent and summed in bfloat16 or wider, within the bound.
No kernel may reach another device: no remote copies, remote signals or barrier semaphores. Data moves between devices by JAX's collectives and lax.ppermute only.
A program may use at most 64 MiB of HBM per device.

v0:
```python
import jax
import jax.numpy as jnp
from jax import lax
from jax.sharding import PartitionSpec as P

BLK = 128


epsilon = 1e-05


def padded_2(cells, sides, width):
    for axis, dim in sides:
        count = lax.axis_size(axis)
        head = lax.slice_in_dim(cells, 0, width, axis=dim)
        tail = lax.slice_in_dim(cells, cells.shape[dim] - width, cells.shape[dim], axis=dim)
        cells = jnp.concatenate(
            [
                lax.ppermute(tail, axis, [(i, (i + 1) % count) for i in range(count)]),
                cells,
                lax.ppermute(head, axis, [((i + 1) % count, i) for i in range(count)]),
            ],
            axis=dim,
        )
    return cells


def arrange(beside_all, position, seq_count):
    prev_last = beside_all[:, 0]
    next_first = beside_all[:, 3]
    blank = jnp.zeros_like(prev_last[:, :1])
    rolled_prev = jnp.concatenate([blank, prev_last[:, :-1]], axis=1)
    rolled_next = jnp.concatenate([next_first[:, 1:], blank], axis=1)
    lead_rim = jnp.where((position > 0)[:, None, None, None], prev_last, rolled_prev)
    tail_rim = jnp.where((position < seq_count - 1)[:, None, None, None], next_first, rolled_next)
    return (lead_rim, tail_rim)


def gate_units(hidden, live_mask):
    channels = hidden.shape[-1] // 2
    gate_half = hidden[:, :channels]
    value_half = hidden[:, channels:]
    return jnp.where(live_mask, gate_half * jax.nn.sigmoid(value_half), 0.0).astype(jnp.bfloat16)


def edge_rows(blocks_arr, margin):
    return jnp.stack([blocks_arr[:, :, :margin], blocks_arr[:, :, BLK - margin :]], axis=1)


def on_device(frames, lengths, owner_map, norm_gain, norm_bias, proj_weight, dw_kernel, out_grad):
    utterances, frame_rows, channels = frames.shape
    block_count = frame_rows // BLK
    tap_count = dw_kernel.shape[0]
    margin = (tap_count - 1) // 2
    seq_count = lax.axis_size("seq")
    seq_index = lax.axis_index("seq")
    position = jnp.mod(seq_index - owner_map[:, 0], seq_count)
    slot_ids = jnp.arange(block_count, dtype=jnp.int32)
    block_id = slot_ids[None, :] * seq_count + position[:, None]
    offsets = jnp.arange(BLK, dtype=jnp.int32)
    frame_id = block_id[:, :, None] * BLK + offsets[None, None, :]
    live_mask = (frame_id < lengths[:, None, None])[..., None]
    frames_wide = frames.reshape(-1, channels).astype(jnp.float32)
    mean_row = jnp.mean(frames_wide, axis=1, keepdims=True)
    centered = frames_wide - mean_row
    inv_std = lax.rsqrt(jnp.mean(centered * centered, axis=1, keepdims=True) + epsilon)
    standard = centered * inv_std
    normed = (standard * norm_gain + norm_bias).astype(jnp.bfloat16)
    weight_full = lax.all_gather(proj_weight, "dp", axis=0, tiled=True)
    hidden = jnp.dot(normed, weight_full, preferred_element_type=jnp.float32)
    gated = gate_units(hidden, live_mask.reshape(-1, 1)).reshape(
        utterances, block_count, BLK, channels
    )
    beside_all = padded_2(edge_rows(gated, margin), (("seq", 1),), 1)
    lead_rim, tail_rim = arrange(beside_all, position, seq_count)
    padded = jnp.concatenate([lead_rim, gated, tail_rim], axis=2)
    conv_out = jnp.zeros((utterances, block_count, BLK, channels), jnp.float32)
    for kernel_tap in range(tap_count):
        conv_out = conv_out + padded[:, :, kernel_tap : kernel_tap + BLK] * dw_kernel[kernel_tap]
    conv_sig = jax.nn.sigmoid(conv_out)
    activations = jnp.where(live_mask, conv_out * conv_sig, 0.0).astype(jnp.bfloat16)
    grad_grid = out_grad.reshape(utterances, block_count, BLK, channels)
    slope = jnp.where(
        live_mask, grad_grid * (conv_sig + conv_out * conv_sig * (1.0 - conv_sig)), 0.0
    ).astype(jnp.bfloat16)
    slope_around = padded_2(edge_rows(slope, margin), (("seq", 1),), 1)
    slope_lead, slope_tail = arrange(slope_around, position, seq_count)
    padded_slope = jnp.concatenate([slope_lead, slope, slope_tail], axis=2)
    slope_wide = slope.astype(jnp.float32)
    kernel_terms = []
    back_sum = jnp.zeros((utterances, block_count, BLK, channels), jnp.float32)
    for kernel_tap in range(tap_count):
        kernel_terms.append(
            jnp.sum(slope_wide * padded[:, :, kernel_tap : kernel_tap + BLK], axis=(0, 1, 2))
        )
        start_row = 2 * margin - kernel_tap
        back_sum = (
            back_sum + padded_slope[:, :, start_row : start_row + BLK] * dw_kernel[kernel_tap]
        )
    kernel_part = jnp.stack(kernel_terms)
    back_flat = jnp.where(live_mask, back_sum, 0.0).reshape(-1, channels)
    gate_half = hidden[:, :channels]
    value_sig = jax.nn.sigmoid(hidden[:, channels:])
    grad_hidden = jnp.concatenate(
        [back_flat * value_sig, back_flat * gate_half * value_sig * (1.0 - value_sig)], axis=1
    ).astype(jnp.bfloat16)
    grad_normed = lax.dot_general(
        grad_hidden, weight_full, (((1,), (1,)), ((), ())), preferred_element_type=jnp.float32
    )
    gain_part = jnp.sum(grad_normed * standard, axis=0)
    bias_part = jnp.sum(grad_normed, axis=0)
    kernel_grad, gain_grad, bias_grad = lax.psum((kernel_part, gain_part, bias_part), ("dp", "seq"))
    scaled = grad_normed * norm_gain
    grad_x = inv_std * (
        scaled
        - jnp.mean(scaled, axis=1, keepdims=True)
        - standard * jnp.mean(scaled * standard, axis=1, keepdims=True)
    )
    input_grad = grad_x.astype(jnp.bfloat16).reshape(utterances, frame_rows, channels)
    return (
        activations.reshape(utterances, frame_rows, channels),
        input_grad,
        kernel_grad,
        gain_grad,
        bias_grad,
    )


def solution(mesh):
    return jax.shard_map(
        on_device,
        mesh=mesh,
        in_specs=(
            P("dp", "seq", None),
            P("dp"),
            P("dp", None),
            P(),
            P(),
            P("dp", None),
            P(),
            P("dp", "seq", None),
        ),
        out_specs=(P("dp", "seq", None), P("dp", "seq", None), P(), P(), P()),
        check_vma=False,
    )
```

profile of v0, /device:TPU:1, one launch (start us, length us, event | category | flops | bytes accessed | tf_op | source)
XLA Modules:
  0.0 728.5 jit_solution(18084784167090012151)
XLA Ops:
  7.2 0.7 all-gather.2.cloned.1.call-update
  9.3 1.8 slice_reduce_fusion.30
  11.1 1.3 convert_reduce_fusion
  13.0 188.6 %all-gather.2.cloned.1.call-done = bf16[1536,3072]{1,0:T(8,128)(2,1)} async-done(((bf16[96,3072]{1,0:T(8,128)(2,1)}), bf16[1536,3072]{1,0:T(8,128)(2,1)}) %all-gather.2.cloned.1.call-update) | async-done | bytes 9437200 | tf_op jit(solution)/shard_map/all_gather | solution.py:69
  201.6 5.5 fusion.108
  207.6 2.1 collective-permute-start
  209.7 12.1 %collective-permute-start.1 = (bf16[1,1,2,15,1536]{4,3,2,1,0:T(8,128)(2,1)S(1)}, bf16[1,1,2,15,1536]{4,3,2,1,0:T(8,128)(2,1)S(1)}, u32[]{:S(2)}, u32[]{:S(2)}) collective-permute-start(bf16[1,1,2,15,1536]{4,3,2,1,0:T(8,128)(2,1)S(1)} %get-tuple-element.80), channel_id=1, source_target_pairs={{1,0},{2,1},{3,2},{4,3},{5,4},{6,5},{7,6},{8,7},{9,8},{10,9},{11,1... | collective-permute-start | bytes 276488 | tf_op jit(solution)/shard_map/ppermute | solution.py:21
  221.7 1.5 slice_reduce_fusion.29
  223.4 11.1 %fusion.91 = (f32[1536]{0:T(1024)S(1)}, f32[1536]{0:T(1024)S(1)}, f32[1536]{0:T(1024)S(1)}, f32[1536]{0:T(1024)S(1)}, f32[1536]{0:T(1024)S(1)}, /*index=5*/f32[1...) fusion(bf16[1,2,15,1536]{3,2,1,0:T(8,128)(2,1)S(1)} %get-tuple-, ...), kind=kLoop, calls=%fused_computation.212 | loop fusion | flops 95930880 | bytes 4362496 | tf_op jit(solution)/shard_map/reduce_sum | solution.py:94
  234.5 2.4 fusion.90
  236.9 1.6 fusion.74
  238.5 2.2 fusion.75
  259.2 6.0 stack.143
  265.3 12.9 %collective-permute-start.2 = (bf16[1,1,2,15,1536]{4,3,2,1,0:T(8,128)(2,1)S(1)}, bf16[1,1,2,15,1536]{4,3,2,1,0:T(8,128)(2,1)S(1)}, u32[]{:S(2)}, u32[]{:S(2)}) collective-permute-start(bf16[1,1,2,15,1536]{4,3,2,1,0:T(8,128)(2,1)S(1)} %get-tuple-element.77), channel_id=1, source_target_pairs={{1,0},{2,1},{3,2},{4,3},{5,4},{6,5},{7,6},{8,7},{9,8},{10,9},{11,1... | collective-permute-start | bytes 276488 | tf_op jit(solution)/shard_map/ppermute | solution.py:21
  278.2 2.1 collective-permute-start.3
  280.3 2.7 select_convert_fusion
  283.0 9.3 %collective-permute-done.3 = bf16[1,1,2,15,1536]{4,3,2,1,0:T(8,128)(2,1)S(1)} collective-permute-done((bf16[1,1,2,15,1536]{4,3,2,1,0:T(8,128)(2,1)S(1)}, bf16[1,1,2,15,1536]{4,3,2,1,0:T(8,128)(2,1)S(1)}, u32[]{:S(2)}, u32[]{:S(2)}) %collective-permute-start.3) | collective-permute-done | bytes 92192 | tf_op jit(solution)/shard_map/ppermute | solution.py:19
  292.4 7.4 %fusion.105 = f32[1,2,128,1536]{3,2,1,0:T(8,128)S(1)} fusion(bf16[1,2,128,1536]{3,2,1,0:T(8,128)(2,1)S(1)} %copy-done.1, bf16[1,2,15,1536]{3,2,1,0:T(8,128)(2,1)S(1)} %pad_select_fusion, bf16[1,2,15,1536]{3,2,1,0:T(8,128)(2,1)S(1)} %pad_select_fusion.1, f32[1536]{0:T(1024)S(1)} %copy-done.12, f32[1536]{0:T(1024)S(1)} %copy-done.14, ...), kind=kLoop, calls=%fused_computation.233 | loop fusion | flops 71958528 | bytes 2734336 | tf_op jit(solution)/shard_map/jit(_where)/select_n | solution.py:101
  299.9 0.8 fusion.101
  301.0 6.8 fusion.13
  307.8 1.4 fusion.107
  309.2 101.2 %all-reduce.4 = (f32[1536]{0:T(1024)}, f32[1536]{0:T(1024)}) all-reduce(f32[1536]{0:T(1024)S(1)} %get-tuple-element.5, f32[1536]{0:T(1024)S(1)} %get-tuple-element.38), channel_id=1, replica_groups=mesh['dp'=16,'seq'=32] {'dp','seq'}, use_global_device_ids=true, to_apply=%region_37.38 | all-reduce | flops 3072 | bytes 24576 | tf_op jit(solution)/shard_map/psum | solution.py:112
  410.5 309.5 %all-reduce.7.cloned.1.call-done = f32[31,1536]{1,0:T(8,128)} async-done(((f32[31,1536]{1,0:T(8,128)}), f32[31,1536]{1,0:T(8,128)}) %all-reduce.7.cloned.1.call-update) | async-done | bytes 190480 | tf_op jit(solution)/shard_map/psum | solution.py:112
  720.0 1.6 copy.15
  (104 shorter events, 20.1 us)
Async XLA Ops:
  7.2 194.4 %copy-start.17 = (f32[1536]{0:T(1024)S(1)}, f32[1536]{0:T(1024)}, u32[]{:S(2)}) copy-start(f32[1536]{0:T(1024)} %param.11) | copy-start | bytes 18436
  7.2 194.4 %copy-start.23 = (f32[1536]{0:T(1024)S(1)}, f32[1536]{0:T(1024)}, u32[]{:S(2)}) copy-start(f32[1536]{0:T(1024)} %param.12) | copy-start | bytes 18436
  7.2 194.4 %all-gather.2.cloned.1.call-start = ((), (), s32[]{:S(2)}) async-start(), calls=%async_computation | async-start | bytes 10027008 | tf_op jit(solution)/shard_map/all_gather | solution.py:69
  7.9 712.1 %all-reduce.7.cloned.1.call-start = ((), (), s32[]{:S(2)}) async-start(), calls=%async_computation.1 | async-start | bytes 393216 | tf_op jit(solution)/shard_map/psum | solution.py:112
  12.4 194.7 %copy-start.15 = (f32[256]{0:T(256)}, f32[256]{0:T(256)S(1)}, u32[]{:S(2)}) copy-start(f32[256]{0:T(256)S(1)} %broadcast_multiply_fusion.2) | copy-start | bytes 3076
  12.9 210.5 %copy-start.19 = (pred[2,128]{1,0:T(4,128)(4,1)}, pred[2,128]{1,0:T(4,128)(4,1)S(1)}, u32[]{:S(2)}) copy-start(pred[2,128]{1,0:T(4,128)(4,1)S(1)} %add_compare_fusion) | copy-start | bytes 772
  13.0 194.1 %copy-start.21 = (f32[256]{0:T(256)}, f32[256]{0:T(256)S(1)}, u32[]{:S(2)}) copy-start(f32[256]{0:T(256)S(1)} %add_rsqrt_fusion) | copy-start | bytes 3076
  207.5 15.8 %copy-start.4 = (bf16[1,256,1536]{2,1,0:T(8,128)(2,1)S(1)}, bf16[1,256,1536]{2,1,0:T(8,128)(2,1)}, u32[]{:S(2)}) copy-start(bf16[1,256,1536]{2,1,0:T(8,128)(2,1)} %param.15) | copy-start | bytes 2359300
  207.6 15.7 %collective-permute-start = (bf16[1,1,2,15,1536]{4,3,2,1,0:T(8,128)(2,1)S(1)}, bf16[1,1,2,15,1536]{4,3,2,1,0:T(8,128)(2,1)S(1)}, u32[]{:S(2)}, u32[]{:S(2)}) collective-permute-start(bf16[1,1,2,15,1536]{4,3,2,1,0:T(8,128)(2,1)S(1)} %get-tuple-element.79), channel_id=1, source_target_pairs={{0,1},{1,2},{2,3},{3,4},{4,5},{5,6},{6,7},{7,8},{8,9},{9,10},{10,1... | collective-permute-start | bytes 276488 | tf_op jit(solution)/shard_map/ppermute | solution.py:19
  209.7 13.7 %collective-permute-start.1 = (bf16[1,1,2,15,1536]{4,3,2,1,0:T(8,128)(2,1)S(1)}, bf16[1,1,2,15,1536]{4,3,2,1,0:T(8,128)(2,1)S(1)}, u32[]{:S(2)}, u32[]{:S(2)}) collective-permute-start(bf16[1,1,2,15,1536]{4,3,2,1,0:T(8,128)(2,1)S(1)} %get-tuple-element.80), channel_id=1, source_target_pairs={{1,0},{2,1},{3,2},{4,3},{5,4},{6,5},{7,6},{8,7},{9,8},{10,9},{11,1... | collective-permute-start | bytes 276488 | tf_op jit(solution)/shard_map/ppermute | solution.py:21
  223.2 11.2 %copy-start.5 = (f32[1536]{0:T(1024)}, f32[1536]{0:T(1024)S(1)}, u32[]{:S(2)}) copy-start(f32[1536]{0:T(1024)S(1)} %get-tuple-element.66) | copy-start | bytes 18436
  223.2 11.2 %copy-start.7 = (f32[1536]{0:T(1024)}, f32[1536]{0:T(1024)S(1)}, u32[]{:S(2)}) copy-start(f32[1536]{0:T(1024)S(1)} %get-tuple-element.67) | copy-start | bytes 18436
  223.3 11.2 %copy-start.9 = (f32[1536]{0:T(1024)}, f32[1536]{0:T(1024)S(1)}, u32[]{:S(2)}) copy-start(f32[1536]{0:T(1024)S(1)} %get-tuple-element.68) | copy-start | bytes 18436
  223.3 11.2 %copy-start.11 = (f32[1536]{0:T(1024)}, f32[1536]{0:T(1024)S(1)}, u32[]{:S(2)}) copy-start(f32[1536]{0:T(1024)S(1)} %get-tuple-element.69) | copy-start | bytes 18436
  223.3 11.2 %copy-start.13 = (f32[1536]{0:T(1024)}, f32[1536]{0:T(1024)S(1)}, u32[]{:S(2)}) copy-start(f32[1536]{0:T(1024)S(1)} %get-tuple-element.70) | copy-start | bytes 18436
  265.2 27.2 %copy-start.1 = (bf16[1,2,128,1536]{3,2,1,0:T(8,128)(2,1)S(1)}, bf16[1,2,128,1536]{3,2,1,0:T(8,128)(2,1)}, u32[]{:S(2)}) copy-start(bf16[1,2,128,1536]{3,2,1,0:T(8,128)(2,1)} %copy-done) | copy-start | bytes 2359300
  265.2 27.2 %copy-start.6 = (f32[1536]{0:T(1024)S(1)}, f32[1536]{0:T(1024)}, u32[]{:S(2)}) copy-start(f32[1536]{0:T(1024)} %copy-done.5) | copy-start | bytes 18436
  265.2 27.2 %copy-start.8 = (f32[1536]{0:T(1024)S(1)}, f32[1536]{0:T(1024)}, u32[]{:S(2)}) copy-start(f32[1536]{0:T(1024)} %copy-done.7) | copy-start | bytes 18436
  265.2 27.2 %copy-start.10 = (f32[1536]{0:T(1024)S(1)}, f32[1536]{0:T(1024)}, u32[]{:S(2)}) copy-start(f32[1536]{0:T(1024)} %copy-done.9) | copy-start | bytes 18436
  265.2 27.2 %copy-start.12 = (f32[1536]{0:T(1024)S(1)}, f32[1536]{0:T(1024)}, u32[]{:S(2)}) copy-start(f32[1536]{0:T(1024)} %copy-done.11) | copy-start | bytes 18436
  265.2 27.2 %copy-start.14 = (f32[1536]{0:T(1024)S(1)}, f32[1536]{0:T(1024)}, u32[]{:S(2)}) copy-start(f32[1536]{0:T(1024)} %copy-done.13) | copy-start | bytes 18436
  265.3 27.2 %copy-start.20 = (pred[2,128]{1,0:T(4,128)(4,1)S(1)}, pred[2,128]{1,0:T(4,128)(4,1)}, u32[]{:S(2)}) copy-start(pred[2,128]{1,0:T(4,128)(4,1)} %copy-done.19) | copy-start | bytes 772
  265.3 17.8 %collective-permute-start.2 = (bf16[1,1,2,15,1536]{4,3,2,1,0:T(8,128)(2,1)S(1)}, bf16[1,1,2,15,1536]{4,3,2,1,0:T(8,128)(2,1)S(1)}, u32[]{:S(2)}, u32[]{:S(2)}) collective-permute-start(bf16[1,1,2,15,1536]{4,3,2,1,0:T(8,128)(2,1)S(1)} %get-tuple-element.77), channel_id=1, source_target_pairs={{1,0},{2,1},{3,2},{4,3},{5,4},{6,5},{7,6},{8,7},{9,8},{10,9},{11,1... | collective-permute-start | bytes 276488 | tf_op jit(solution)/shard_map/ppermute | solution.py:21
  278.2 14.1 %collective-permute-start.3 = (bf16[1,1,2,15,1536]{4,3,2,1,0:T(8,128)(2,1)S(1)}, bf16[1,1,2,15,1536]{4,3,2,1,0:T(8,128)(2,1)S(1)}, u32[]{:S(2)}, u32[]{:S(2)}) collective-permute-start(bf16[1,1,2,15,1536]{4,3,2,1,0:T(8,128)(2,1)S(1)} %get-tuple-element.78), channel_id=1, source_target_pairs={{0,1},{1,2},{2,3},{3,4},{4,5},{5,6},{6,7},{7,8},{8,9},{9,10},{10,1... | collective-permute-start | bytes 276488 | tf_op jit(solution)/shard_map/ppermute | solution.py:19
  (6 other events, 15.9 us)
Sparse Core Ops, SparseCore 0:
  11.3 190.2 all-gather.1
  265.3 454.6 all-reduce.6
where the time goes:
time: 729 us; the launch traced here: 728 us
  waiting for transfers between devices  508 us (70%)
  blocking collectives  101 us (14%)
  other arithmetic  31.8 us (4%)
  local copies, waits for them, and re-layouts  29.9 us (4%)
  starting transfers between devices  29.2 us (4%)
  between operations  15.9 us (2%)
  matrix products  12.3 us (2%)
    psum x1, waiting for transfers between devices, on_device(): lax.psum((kernel_part, gain_part, bias_part), ('dp', 'seq'))  310 us
    all_gather x1, waiting for transfers between devices, on_device(): weight_full = lax.all_gather(proj_weight, 'dp', axis=0, tiled=True)  189 us
    psum x1, blocking collectives, on_device(): lax.psum((kernel_part, gain_part, bias_part), ('dp', 'seq'))  101 us
    ppermute x2, starting transfers between devices, padded_2(): lax.ppermute(head, axis, [((i + 1) % count, i) for i in range(count)])  25 us
    another operation x32, local copies, waits for them, and re-layouts, on_device(): kernel_part = jnp.stack(kernel_terms)  24.4 us
    reduce_sum x4, other arithmetic, on_device(): jnp.sum(slope_wide * padded[:, :, kernel_tap:kernel_tap + BLK], axis=(0,...  17.2 us
  transfers between devices with their start and end apart: 6, of which 3 were waited for; matrix products, arithmetic and copies ran while one was open for 3% of the time, Pallas kernels for 0%

commit v1 on v0

v1 whole, which is shorter than its diff:
```python
import jax
import jax.numpy as jnp
from jax import lax
from jax.experimental import pallas as pl
from jax.experimental.pallas import tpu as pltpu
from jax.sharding import Mesh, PartitionSpec as P

D = 1536
TAPS = 31
BLK = 128
HX = 32
EXT = BLK + 2 * HX
HG = 16
EXG = BLK + 2 * HG
SHARD = 96
QUART = 768
LT = D // 128
SLOT = 40
PACK = 512
EPS = 1e-05
F32 = jnp.float32
BF16 = jnp.bfloat16


def sigmoid(v):
    return 0.5 * jnp.tanh(0.5 * v) + 0.5


def shift(count, by):
    return [(i, (i + by) % count) for i in range(count)]


def fused(sc, x_hbm, og_hbm, hp, hn, gain, bias, dw, own0, own1, own2, own3, oc,
          ya0, ya1, ya2, ya3, yb,
          act_ref, ig_ref, red_ref,
          xe, oge, w, nrm, std, inv, gbuf, abuf, sbuf, slp, wb, kacc, gh, gn,
          xsem, wsem):
    pos, length = sc[0], sc[1]
    zh, xi, ci, yi = sc[2], sc[3], sc[4], sc[5]

    xcopies = []

    def go(src, dst, sem, bag):
        c = pltpu.make_async_copy(src, dst, sem)
        c.start()
        bag.append(c)

    for s in range(2):
        before = jnp.maximum(s - jnp.where(pos == 0, 1, 0), 0)
        after = jnp.minimum(s + jnp.where(pos == 31, 1, 0), 1)
        n = 6 * s
        go(x_hbm.at[pl.ds(s * BLK, BLK)], xe.at[pl.ds(s * EXT + HX, BLK)], xsem.at[n], xcopies)
        go(hp.at[pl.ds(pl.multiple_of(before * HX, HX), HX)], xe.at[pl.ds(s * EXT, HX)], xsem.at[n + 1], xcopies)
        go(hn.at[pl.ds(pl.multiple_of(after * HX, HX), HX)], xe.at[pl.ds(s * EXT + HX + BLK, HX)], xsem.at[n + 2], xcopies)
        go(og_hbm.at[pl.ds(s * BLK, BLK)], oge.at[pl.ds(s * EXG + HG, BLK)], xsem.at[n + 3], xcopies)
        go(hp.at[pl.ds(pl.multiple_of(2 * HX + before * HG, HG), HG)], oge.at[pl.ds(s * EXG, HG)], xsem.at[n + 4], xcopies)
        go(hn.at[pl.ds(pl.multiple_of(2 * HX + after * HG, HG), HG)], oge.at[pl.ds(s * EXG + HG + BLK, HG)], xsem.at[n + 5], xcopies)

    wcopies = []

    def row_of(z, x, c):
        return pl.multiple_of((z * 8 + x * 2 + c) * SHARD, SHARD)

    k = 0
    for r, ref in enumerate((own0, own1, own2, own3)):
        xr = lax.rem(xi + 4 - r, 4)
        go(ref, w.at[pl.ds(row_of(zh, xr, ci), SHARD)], wsem.at[k], wcopies)
        go(oc.at[pl.ds(r * SHARD, SHARD)], w.at[pl.ds(row_of(zh, xr, 1 - ci), SHARD)], wsem.at[k + 1], wcopies)
        k += 2
    for dy, ref in enumerate((ya0, ya1, ya2, ya3)):
        col = pl.multiple_of(lax.rem(yi + 4 - dy, 4) * QUART, QUART)
        for r in range(4):
            xr = lax.rem(xi + 4 - r, 4)
            go(ref.at[pl.ds(r * SHARD, SHARD)], w.at[pl.ds(row_of(1 - zh, xr, ci), SHARD), pl.ds(col, QUART)], wsem.at[k], wcopies)
            go(yb.at[pl.ds((dy * 4 + r) * SHARD, SHARD)], w.at[pl.ds(row_of(1 - zh, xr, 1 - ci), SHARD), pl.ds(col, QUART)], wsem.at[k + 1], wcopies)
            k += 2

    red_ref[...] = jnp.zeros((PACK, 128), F32)
    for c in xcopies:
        c.wait()

    gain_row = gain[...]
    bias_row = bias[...]

    def norm_step(i, carry):
        rows = pl.ds(pl.multiple_of(i * 32, 32), 32)
        v = xe[rows, :].astype(F32)
        mean = jnp.sum(v, axis=1, keepdims=True) * (1.0 / D)
        c = v - mean
        var = jnp.sum(c * c, axis=1, keepdims=True) * (1.0 / D)
        iv = lax.rsqrt(var + EPS)
        st = c * iv
        std[rows, :] = st
        inv[rows, :] = jnp.broadcast_to(iv, (32, 128))
        nrm[rows, :] = (st * gain_row + bias_row).astype(BF16)
        return carry

    lax.fori_loop(0, 2 * EXT // 32, norm_step, 0)

    for c in wcopies:
        c.wait()

    row384 = lax.broadcasted_iota(jnp.int32, (2 * EXT, 128), 0)
    second = row384 >= EXT
    t384 = pos * BLK + jnp.where(second, row384 - EXT + 32 * BLK, row384) - HX
    live384 = (t384 >= 0) & (t384 < length)
    iota16 = lax.broadcasted_iota(jnp.int32, (16, 128), 0)

    def chan_step(j, carry):
        col = pl.multiple_of(j * 256, 256)
        normed = nrm[...]
        a = jnp.dot(normed, w[:, pl.ds(col, 256)], preferred_element_type=F32)
        b = jnp.dot(normed, w[:, pl.ds(D + col, 256)], preferred_element_type=F32)
        sg = sigmoid(b)
        for h in range(2):
            ah = a[:, h * 128:(h + 1) * 128]
            sh = sg[:, h * 128:(h + 1) * 128]
            abuf[h] = ah
            sbuf[h] = sh
            gbuf[h] = jnp.where(live384, ah * sh, 0.0).astype(BF16).astype(F32)

        def tile_step(q, carry2):
            h = q // 2
            s = q % 2
            lane = pl.multiple_of((2 * j + h) * 128, 128)
            first = (pos + 32 * s) * BLK
            ext0 = s * EXT

            @pl.when(s == 0)
            def _():
                for k in range(TAPS):
                    wb[k] = jnp.broadcast_to(dw[pl.ds(k, 1), pl.ds(lane, 128)], (8, 128))
                    kacc[k] = jnp.zeros((8, 128), F32)

            taps = [wb[k] for k in range(TAPS)]
            acc = {}
            done = {}
            for o in range(1, 8 * 19 + 32):
                v = gbuf[h, pl.ds(ext0 + o, 8), :]
                for i in range(20):
                    k = o - 1 - 8 * i
                    if 0 <= k < TAPS:
                        p = v * taps[k]
                        acc[i] = p if k == 0 else acc[i] + p
                        if k == TAPS - 1:
                            done[i] = acc.pop(i)
                            if i % 2 == 1:
                                m = i // 2
                                conv = jnp.concatenate([done.pop(i - 1), done.pop(i)], axis=0)
                                cs = sigmoid(conv)
                                t = iota16 + (first + 16 * m - HG)
                                live = (t >= 0) & (t < length)
                                og = oge[pl.ds(pl.multiple_of(s * EXG + 16 * m, 16), 16), pl.ds(lane, 128)].astype(F32)
                                av = conv * cs
                                sl = jnp.where(live, og * (cs + av * (1.0 - cs)), 0.0).astype(BF16).astype(F32)
                                slp[pl.ds(16 * m, 16), :] = sl
                                if 1 <= m <= 8:
                                    act_ref[pl.ds(pl.multiple_of(s * BLK + 16 * (m - 1), 16), 16), pl.ds(lane, 128)] = (
                                        jnp.where(live, av, 0.0).astype(BF16))

            ks = [kacc[k] for k in range(TAPS)]
            sv = {}
            for o in range(17, 17 + 8 * 15 + TAPS):
                v = gbuf[h, pl.ds(ext0 + o, 8), :]
                for i in range(16):
                    k = o - 17 - 8 * i
                    if 0 <= k < TAPS:
                        if k == 0:
                            sv[i] = slp[pl.ds(16 + 8 * i, 8), :]
                        ks[k] = ks[k] + v * sv[i]
            for k in range(TAPS):
                kacc[k] = ks[k]

            @pl.when(s == 1)
            def _():
                for k in range(TAPS):
                    red_ref[pl.ds((2 * j + h) * SLOT + k, 1), :] = jnp.sum(ks[k], axis=0, keepdims=True)

            acc = {}
            done = {}
            for o in range(1, 8 * 15 + 32):
                v = slp[pl.ds(o, 8), :]
                for i in range(16):
                    k = 31 + 8 * i - o
                    if 0 <= k < TAPS:
                        p = v * taps[k]
                        acc[i] = p if k == TAPS - 1 else acc[i] + p
                        if k == 0:
                            done[i] = acc.pop(i)
                            if i % 2 == 1:
                                m = i // 2
                                back = jnp.concatenate([done.pop(i - 1), done.pop(i)], axis=0)
                                t = iota16 + (first + 16 * m)
                                back = jnp.where(t < length, back, 0.0)
                                rows = pl.ds(pl.multiple_of(ext0 + HX + 16 * m, 16), 16)
                                av = abuf[h, rows, :]
                                sgv = sbuf[h, rows, :]
                                ga = back * sgv
                                out = pl.ds(pl.multiple_of(s * BLK + 16 * m, 16), 16)
                                gh[out, pl.ds(lane, 128)] = ga.astype(BF16)
                                gh[out, pl.ds(D + lane, 128)] = (ga * av * (1.0 - sgv)).astype(BF16)
            return carry2

        lax.fori_loop(0, 4, tile_step, 0)
        return carry

    lax.fori_loop(0, D // 256, chan_step, 0)

    def back_step(n, carry):
        rows = pl.ds(pl.multiple_of(n * 256, 256), 256)
        gn[:, rows] = lax.dot_general(gh[...], w[rows, :], (((1,), (1,)), ((), ())), preferred_element_type=F32)
        return carry

    lax.fori_loop(0, D // 256, back_step, 0)

    def grad_step(i, carry):
        gsum, bsum = carry
        src = pl.ds(pl.multiple_of(jnp.where(i >= 4, EXT - BLK, 0) + HX + i * 32, 32), 32)
        dst = pl.ds(pl.multiple_of(i * 32, 32), 32)
        g = gn[dst, :]
        st = std[src, :]
        gs = g * st
        for q in range(4):
            gsum = gsum + gs[q * 8:(q + 1) * 8]
            bsum = bsum + g[q * 8:(q + 1) * 8]
        sc_ = g * gain_row
        m1 = jnp.sum(sc_, axis=1, keepdims=True) * (1.0 / D)
        m2 = jnp.sum(sc_ * st, axis=1, keepdims=True) * (1.0 / D)
        iv = inv[src, 0:1]
        ig_ref[dst, :] = (iv * (sc_ - m1 - st * m2)).astype(BF16)
        return gsum, bsum

    zero = jnp.zeros((8, D), F32)
    gsum, bsum = lax.fori_loop(0, 8, grad_step, (zero, zero))
    grow = jnp.sum(gsum, axis=0, keepdims=True)
    brow = jnp.sum(bsum, axis=0, keepdims=True)
    for l in range(LT):
        red_ref[l * SLOT + TAPS:l * SLOT + TAPS + 1, :] = grow[:, l * 128:(l + 1) * 128]
        red_ref[l * SLOT + TAPS + 1:l * SLOT + TAPS + 2, :] = brow[:, l * 128:(l + 1) * 128]


def run_fused(scalars, frames, out_grad, hp, hn, gain, bias, dw, pieces):
    any_spec = pl.BlockSpec(memory_space=pl.ANY)
    vm = pl.BlockSpec(memory_space=pltpu.VMEM)
    return pl.pallas_call(
        fused,
        out_shape=(
            jax.ShapeDtypeStruct((2 * BLK, D), BF16),
            jax.ShapeDtypeStruct((2 * BLK, D), BF16),
            jax.ShapeDtypeStruct((PACK, 128), F32),
        ),
        in_specs=[pl.BlockSpec(memory_space=pltpu.SMEM)] + [any_spec] * 4 + [vm] * 3 + [any_spec] * len(pieces),
        out_specs=(vm, vm, vm),
        scratch_shapes=[
            pltpu.VMEM((2 * EXT, D), BF16),
            pltpu.VMEM((2 * EXG, D), BF16),
            pltpu.VMEM((D, 2 * D), BF16),
            pltpu.VMEM((2 * EXT, D), BF16),
            pltpu.VMEM((2 * EXT, D), F32),
            pltpu.VMEM((2 * EXT, 128), F32),
            pltpu.VMEM((2, 2 * EXT, 128), F32),
            pltpu.VMEM((2, 2 * EXT, 128), F32),
            pltpu.VMEM((2, 2 * EXT, 128), F32),
            pltpu.VMEM((EXG, 128), F32),
            pltpu.VMEM((TAPS, 8, 128), F32),
            pltpu.VMEM((TAPS, 8, 128), F32),
            pltpu.VMEM((2 * BLK, 2 * D), BF16),
            pltpu.VMEM((2 * BLK, D), F32),
            pltpu.SemaphoreType.DMA((12,)),
            pltpu.SemaphoreType.DMA((40,)),
        ],
        compiler_params=pltpu.CompilerParams(vmem_limit_bytes=48 * 1024 * 1024),
        cost_estimate=pl.CostEstimate(flops=9_000_000_000, bytes_accessed=14_000_000, transcendentals=2_000_000),
    )(scalars, frames, out_grad, hp, hn, gain, bias, dw, *pieces)


def gather_weight(own):
    yi = lax.axis_index("y")
    quarter = lax.dynamic_slice_in_dim(own, yi * QUART, QUART, axis=1)
    far = lax.ppermute(quarter, "zh", shift(2, 1))
    far = [far] + [lax.ppermute(far, "x", shift(4, d)) for d in (1, 2, 3)]
    far = jnp.concatenate(far, axis=0)
    ya = [far] + [lax.ppermute(far, "y", shift(4, d)) for d in (1, 2, 3)]
    mine = [own] + [lax.ppermute(own, "x", shift(4, d)) for d in (1, 2, 3)]
    oc = lax.ppermute(jnp.concatenate(mine, axis=0), "core", shift(2, 1))
    yb = lax.ppermute(jnp.concatenate(ya, axis=0), "core", shift(2, 1))
    return mine + [oc] + ya + [yb]


def reduce_all(packed):
    plane = ("x", "core", "y")
    parts = lax.all_to_all(packed.reshape(32, PACK // 32, 128), plane, 0, 0)
    mine = jnp.sum(parts, axis=0)
    line = lax.all_to_all(jnp.broadcast_to(mine[None], (16,) + mine.shape), ("zh", "zl"), 0, 0)
    mine = jnp.sum(line, axis=0)
    whole = lax.all_to_all(jnp.broadcast_to(mine[None], (32,) + mine.shape), plane, 0, 0)
    whole = whole.reshape(PACK, 128)[: LT * SLOT].reshape(LT, SLOT, 128)
    whole = jnp.swapaxes(whole, 0, 1).reshape(SLOT, D)
    return whole[:TAPS], whole[TAPS], whole[TAPS + 1]


def on_device(frames, lengths, owner_map, norm_gain, norm_bias, proj_weight, dw_kernel, out_grad):
    idx = lax.axis_index
    x = frames.reshape(2 * BLK, D)
    dy = out_grad.reshape(2 * BLK, D)
    seq = idx("y") * 8 + idx("zl")
    position = jnp.mod(seq - owner_map[0, 0], 32)
    scalars = jnp.stack([position, lengths[0], idx("zh"), idx("x"), idx("core"), idx("y"), position, position]).astype(jnp.int32)

    tails = jnp.concatenate([x[BLK - HX:BLK], x[2 * BLK - HX:], dy[BLK - HG:BLK], dy[2 * BLK - HG:]], axis=0)
    heads = jnp.concatenate([x[:HX], x[BLK:BLK + HX], dy[:HG], dy[BLK:BLK + HG]], axis=0)
    pieces = gather_weight(proj_weight)
    hp = lax.ppermute(tails, ("y", "zl"), shift(32, 1))
    hn = lax.ppermute(heads, ("y", "zl"), shift(32, -1))
    act, ig, packed = run_fused(
        scalars, x, dy, hp, hn, norm_gain.reshape(1, D), norm_bias.reshape(1, D), dw_kernel, pieces)
    kernel_grad, gain_grad, bias_grad = reduce_all(packed)
    return act.reshape(1, 2 * BLK, D), ig.reshape(1, 2 * BLK, D), kernel_grad, gain_grad, bias_grad


def solution(mesh):
    fine = Mesh(mesh.devices.reshape(2, 4, 2, 4, 8), ("zh", "x", "core", "y", "zl"))
    dp, seq = ("zh", "x", "core"), ("y", "zl")
    return jax.shard_map(
        on_device,
        mesh=fine,
        in_specs=(P(dp, seq, None), P(dp), P(dp, None), P(), P(), P(dp, None), P(), P(dp, seq, None)),
        out_specs=(P(dp, seq, None), P(dp, seq, None), P(), P(), P()),
        check_vma=False,
    )
```

time: 729 us -> 225 us (0.31)
  waiting for transfers between devices: 508 us -> 56.1 us
  blocking collectives: 101 us -> 51.6 us
  starting transfers between devices: 29.2 us -> 67.8 us
  Pallas kernels: 0 us -> 29.1 us
  other arithmetic: 31.8 us -> 3.14 us
  local copies, waits for them, and re-layouts: 29.9 us -> 14.6 us
  between operations: 15.9 us -> 1.63 us
  matrix products: 12.3 us -> 0 us
    psum x1 -> x0, waiting for transfers between devices: 310 us -> none  [on_device(): lax.psum((kernel_part, gain_part, bias_part), ('dp', 'seq'))]
    all_gather x1 -> x0, waiting for transfers between devices: 189 us -> none  [on_device(): weight_full = lax.all_gather(proj_weight, 'dp', axis=0, tiled=True)]
    psum x1 -> x0, blocking collectives: 101 us -> none  [on_device(): lax.psum((kernel_part, gain_part, bias_part), ('dp', 'seq'))]
    all_to_all x0 -> x3, blocking collectives: none -> 51.6 us  [the longest x1 20.2 us: reduce_all(): lax.all_to_all(jnp.broadcast_to(mine[None], (16,) + mine.shape), ('zh', '...]
    ppermute x4 -> x14, waiting for transfers between devices: 9.31 us -> 56.1 us  [the longest x3 20.3 us: gather_weight(): far = [far] + [lax.ppermute(far, 'x', shift(4, d)) for d in (1, 2, 3)]]
    ppermute x4 -> x14, starting transfers between devices: 29.1 us -> 67.8 us  [the longest x1 16.3 us: gather_weight(): far = lax.ppermute(quarter, 'zh', shift(2, 1))]
    pallas_call x0 -> x1, Pallas kernels: none -> 29.1 us  [run_fused(): pl.pallas_call(fused, out_shape=(jax.ShapeDtypeStruct((2 * BLK, D), BF16)...]
    another operation x34 -> x1, local copies, waits for them, and re-layouts: 24.5 us -> 0.57 us  [on_device(): jnp.stack([position, lengths[0], idx('zh'), idx('x'), idx('core'), idx('y...]
  transfers between devices with their start and end apart: 6 -> 14, of which waited for: 3 -> 7; matrix products, arithmetic and copies ran while one was open for 3% -> 5% of each run, Pallas kernels for 0% -> 0%
where the time goes in v1:
time: 225 us; the launch traced here: 224 us
  starting transfers between devices  67.8 us (30%)
  waiting for transfers between devices  56.1 us (25%)
  blocking collectives  51.6 us (23%)
  Pallas kernels  29.1 us (13%)
  local copies, waits for them, and re-layouts  14.6 us (6%)
  other arithmetic  3.14 us (1%)
    pallas_call x1, Pallas kernels, run_fused(): pl.pallas_call(fused, out_shape=(jax.ShapeDtypeStruct((2 * BLK, D), BF16)...  29.1 us
    ppermute x3, waiting for transfers between devices, gather_weight(): far = [far] + [lax.ppermute(far, 'x', shift(4, d)) for d in (1, 2, 3)]  20.3 us
    all_to_all x1, blocking collectives, reduce_all(): lax.all_to_all(jnp.broadcast_to(mine[None], (16,) + mine.shape), ('zh', '...  20.2 us
    ppermute x1, starting transfers between devices, gather_weight(): far = lax.ppermute(quarter, 'zh', shift(2, 1))  16.3 us
    all_to_all x1, blocking collectives, reduce_all(): parts = lax.all_to_all(packed.reshape(32, PACK // 32, 128), plane, 0, 0)  16 us
    all_to_all x1, blocking collectives, reduce_all(): lax.all_to_all(jnp.broadcast_to(mine[None], (32,) + mine.shape), plane, 0...  15.4 us
    ppermute x1, waiting for transfers between devices, on_device(): hp = lax.ppermute(tails, ('y', 'zl'), shift(32, 1))  15.1 us
    ppermute x3, waiting for transfers between devices, gather_weight(): ya = [far] + [lax.ppermute(far, 'y', shift(4, d)) for d in (1, 2, 3)]  13.8 us
  transfers between devices with their start and end apart: 14, of which 7 were waited for; matrix products, arithmetic and copies ran while one was open for 5% of the time, Pallas kernels for 0%

profile of v1, /device:TPU:1, one launch (start us, length us, event | category | flops | bytes accessed | tf_op | source)
XLA Modules:
  0.0 224.0 jit_solution(6478098823658131236)
XLA Ops:
  1.6 16.3 %collective-permute-start.6 = (bf16[96,768]{1,0:T(8,128)(2,1)S(1)}, bf16[96,768]{1,0:T(8,128)(2,1)S(1)}, u32[]{:S(2)}, u32[]{:S(2)}) collective-permute-start(bf16[96,768]{1,0:T(8,128)(2,1)S(1)} %constant_dynamic-slice_fusion), channel_id=1, source_target_pairs={{0,256},{256,0},{1,257},{257,1},{2,258},{258,2},{3,259},{259,3},{4... | collective-permute-start | bytes 442376 | tf_op jit(solution)/shard_map/ppermute | solution.py:280
  17.9 4.0 %collective-permute-done.6 = bf16[96,768]{1,0:T(8,128)(2,1)S(1)} collective-permute-done((bf16[96,768]{1,0:T(8,128)(2,1)S(1)}, bf16[96,768]{1,0:T(8,128)(2,1)S(1)}, u32[]{:S(2)}, u32[]{:S(2)}) %collective-permute-start.6) | collective-permute-done | bytes 147488 | tf_op jit(solution)/shard_map/ppermute | solution.py:280
  21.9 2.7 %collective-permute-start.7 = (bf16[96,768]{1,0:T(8,128)(2,1)S(1)}, bf16[96,768]{1,0:T(8,128)(2,1)S(1)}, u32[]{:S(2)}, u32[]{:S(2)}) collective-permute-start(bf16[96,768]{1,0:T(8,128)(2,1)S(1)} %collective-permute-done.6), channel_id=1, source_target_pairs={{0,64},{64,128},{128,192},{192,0},{1,65},{65,129},{129,193},{193,1... | collective-permute-start | bytes 442376 | tf_op jit(solution)/shard_map/ppermute | solution.py:281
  24.6 3.1 %collective-permute-start.2 = (bf16[96,3072]{1,0:T(8,128)(2,1)}, bf16[96,3072]{1,0:T(8,128)(2,1)S(1)}, u32[]{:S(2)}, u32[]{:S(2)}) collective-permute-start(bf16[96,3072]{1,0:T(8,128)(2,1)} %own0.1), channel_id=1, source_target_pairs={{0,64},{64,128},{128,192},{192,0},{1,65},{65,129},{129,193},{193,1... | collective-permute-start | bytes 1769480 | tf_op jit(solution)/shard_map/ppermute | solution.py:284
  27.7 3.8 %collective-permute-start.3 = (bf16[96,3072]{1,0:T(8,128)(2,1)}, bf16[96,3072]{1,0:T(8,128)(2,1)S(1)}, u32[]{:S(2)}, u32[]{:S(2)}) collective-permute-start(bf16[96,3072]{1,0:T(8,128)(2,1)} %own0.1), channel_id=1, source_target_pairs={{0,128},{64,192},{128,0},{192,64},{1,129},{65,193},{129,1},{193,65... | collective-permute-start | bytes 1769480 | tf_op jit(solution)/shard_map/ppermute | solution.py:284
  31.5 3.4 %collective-permute-start.4 = (bf16[96,3072]{1,0:T(8,128)(2,1)}, bf16[96,3072]{1,0:T(8,128)(2,1)S(1)}, u32[]{:S(2)}, u32[]{:S(2)}) collective-permute-start(bf16[96,3072]{1,0:T(8,128)(2,1)} %own0.1), channel_id=1, source_target_pairs={{0,192},{64,0},{128,64},{192,128},{1,193},{65,1},{129,65},{193,129... | collective-permute-start | bytes 1769480 | tf_op jit(solution)/shard_map/ppermute | solution.py:284
  34.9 2.4 %collective-permute-start.8 = (bf16[96,768]{1,0:T(8,128)(2,1)S(1)}, bf16[96,768]{1,0:T(8,128)(2,1)S(1)}, u32[]{:S(2)}, u32[]{:S(2)}) collective-permute-start(bf16[96,768]{1,0:T(8,128)(2,1)S(1)} %collective-permute-done.6), channel_id=1, source_target_pairs={{0,128},{64,192},{128,0},{192,64},{1,129},{65,193},{129,1},{193,65... | collective-permute-start | bytes 442376 | tf_op jit(solution)/shard_map/ppermute | solution.py:281
  38.0 3.8 %collective-permute-start.9 = (bf16[96,768]{1,0:T(8,128)(2,1)S(1)}, bf16[96,768]{1,0:T(8,128)(2,1)S(1)}, u32[]{:S(2)}, u32[]{:S(2)}) collective-permute-start(bf16[96,768]{1,0:T(8,128)(2,1)S(1)} %collective-permute-done.6), channel_id=1, source_target_pairs={{0,192},{64,0},{128,64},{192,128},{1,193},{65,1},{129,65},{193,129... | collective-permute-start | bytes 442376 | tf_op jit(solution)/shard_map/ppermute | solution.py:281
  42.5 15.2 %collective-permute-done.8 = bf16[96,768]{1,0:T(8,128)(2,1)S(1)} collective-permute-done((bf16[96,768]{1,0:T(8,128)(2,1)S(1)}, bf16[96,768]{1,0:T(8,128)(2,1)S(1)}, u32[]{:S(2)}, u32[]{:S(2)}) %collective-permute-start.8) | collective-permute-done | bytes 147488 | tf_op jit(solution)/shard_map/ppermute | solution.py:281
  58.3 5.1 %collective-permute-done.9 = bf16[96,768]{1,0:T(8,128)(2,1)S(1)} collective-permute-done((bf16[96,768]{1,0:T(8,128)(2,1)S(1)}, bf16[96,768]{1,0:T(8,128)(2,1)S(1)}, u32[]{:S(2)}, u32[]{:S(2)}) %collective-permute-start.9) | collective-permute-done | bytes 147488 | tf_op jit(solution)/shard_map/ppermute | solution.py:281
  64.1 3.2 %collective-permute-start.10 = (bf16[384,768]{1,0:T(8,128)(2,1)S(1)}, bf16[384,768]{1,0:T(8,128)(2,1)S(1)}, u32[]{:S(2)}, u32[]{:S(2)}) collective-permute-start(bf16[384,768]{1,0:T(8,128)(2,1)S(1)} %get-tuple-element.22.ya0), channel_id=1, source_target_pairs={{0,8},{8,16},{16,24},{24,0},{1,9},{9,17},{17,25},{25,1},{2,10},{10... | collective-permute-start | bytes 1769480 | tf_op jit(solution)/shard_map/ppermute | solution.py:283
  67.3 4.5 %collective-permute-start.11 = (bf16[384,768]{1,0:T(8,128)(2,1)S(1)}, bf16[384,768]{1,0:T(8,128)(2,1)S(1)}, u32[]{:S(2)}, u32[]{:S(2)}) collective-permute-start(bf16[384,768]{1,0:T(8,128)(2,1)S(1)} %get-tuple-element.22.ya0), channel_id=1, source_target_pairs={{0,16},{8,24},{16,0},{24,8},{1,17},{9,25},{17,1},{25,9},{2,18},{10... | collective-permute-start | bytes 1769480 | tf_op jit(solution)/shard_map/ppermute | solution.py:283
  71.9 3.0 %collective-permute-start.12 = (bf16[384,768]{1,0:T(8,128)(2,1)S(1)}, bf16[384,768]{1,0:T(8,128)(2,1)S(1)}, u32[]{:S(2)}, u32[]{:S(2)}) collective-permute-start(bf16[384,768]{1,0:T(8,128)(2,1)S(1)} %get-tuple-element.22.ya0), channel_id=1, source_target_pairs={{0,24},{8,0},{16,8},{24,16},{1,25},{9,1},{17,9},{25,17},{2,26},{10... | collective-permute-start | bytes 1769480 | tf_op jit(solution)/shard_map/ppermute | solution.py:283
  76.5 4.6 %collective-permute-start.5 = (bf16[384,3072]{1,0:T(8,128)(2,1)}, bf16[384,3072]{1,0:T(8,128)(2,1)}, u32[]{:S(2)}, u32[]{:S(2)}) collective-permute-start(bf16[384,3072]{1,0:T(8,128)(2,1)} %pad_maximum_fusion), channel_id=1, source_target_pairs={{0,32},{32,0},{1,33},{33,1},{2,34},{34,2},{3,35},{35,3},{4,36},{36... | collective-permute-start | bytes 7077896 | tf_op jit(solution)/shard_map/ppermute | solution.py:285
  82.0 12.2 %collective-permute-done.11.ya2 = bf16[384,768]{1,0:T(8,128)(2,1)S(1)} collective-permute-done((bf16[384,768]{1,0:T(8,128)(2,1)S(1)}, bf16[384,768]{1,0:T(8,128)(2,1)S(1)}, u32[]{:S(2)}, u32[]{:S(2)}) %collective-permute-start.11) | collective-permute-done | bytes 589856 | tf_op jit(solution)/shard_map/ppermute | solution.py:283
  98.4 3.5 %collective-permute-start.13 = (bf16[1536,768]{1,0:T(8,128)(2,1)}, bf16[1536,768]{1,0:T(8,128)(2,1)}, u32[]{:S(2)}, u32[]{:S(2)}) collective-permute-start(bf16[1536,768]{1,0:T(8,128)(2,1)} %constant_dynamic-update-slice_fusion.4), channel_id=1, source_target_pairs={{0,32},{32,0},{1,33},{33,1},{2,34},{34,2},{3,35},{35,3},{4,36},{36... | collective-permute-start | bytes 7077896 | tf_op jit(solution)/shard_map/ppermute | solution.py:286
  103.5 8.1 %collective-permute-start.1 = (bf16[96,1536]{1,0:T(8,128)(2,1)}, bf16[96,1536]{1,0:T(8,128)(2,1)}, u32[]{:S(2)}, u32[]{:S(2)}) collective-permute-start(bf16[96,1536]{1,0:T(8,128)(2,1)} %pad_maximum_fusion.2), channel_id=1, source_target_pairs={{0,31},{1,0},{2,1},{3,2},{4,3},{5,4},{6,5},{7,6},{8,7},{9,8},{10,9... | collective-permute-start | bytes 884744 | tf_op jit(solution)/shard_map/ppermute | solution.py:314
  112.3 5.6 %collective-permute-start = (bf16[96,1536]{1,0:T(8,128)(2,1)}, bf16[96,1536]{1,0:T(8,128)(2,1)}, u32[]{:S(2)}, u32[]{:S(2)}) collective-permute-start(bf16[96,1536]{1,0:T(8,128)(2,1)} %pad_maximum_fusion.1), channel_id=1, source_target_pairs={{0,1},{1,2},{2,3},{3,4},{4,5},{5,6},{6,7},{7,8},{8,9},{9,10},{10,1... | collective-permute-start | bytes 884744 | tf_op jit(solution)/shard_map/ppermute | solution.py:313
  119.9 3.0 %collective-permute-done.1.hn = bf16[96,1536]{1,0:T(8,128)(2,1)} collective-permute-done((bf16[96,1536]{1,0:T(8,128)(2,1)}, bf16[96,1536]{1,0:T(8,128)(2,1)}, u32[]{:S(2)}, u32[]{:S(2)}) %collective-permute-start.1) | collective-permute-done | bytes 294944 | tf_op jit(solution)/shard_map/ppermute | solution.py:314
  122.9 15.1 %collective-permute-done.hp = bf16[96,1536]{1,0:T(8,128)(2,1)} collective-permute-done((bf16[96,1536]{1,0:T(8,128)(2,1)}, bf16[96,1536]{1,0:T(8,128)(2,1)}, u32[]{:S(2)}, u32[]{:S(2)}) %collective-permute-start) | collective-permute-done | bytes 294944 | tf_op jit(solution)/shard_map/ppermute | solution.py:313
  141.6 29.1 %shard_map.119 = (bf16[256,1536]{1,0:T(8,128)(2,1)}, bf16[256,1536]{1,0:T(8,128)(2,1)}, f32[512,128]{1,0:T(8,128)S(1)}) custom-call(s32[8]{0:T(128)S(1)} %copy-done.5, bf16[256,1536]{1,0:T(8,128)(2,1)} %bitcast.41, bf16[256,1536]{1,0:T(8,128)(2,1)} %bitcast.42, bf16[96,1536]{1,0:T(8,128)(2,1)} %collective-permute-done.hp, ...), custom_call_target="tpu_custom_call" | custom-call | flops 8999999488 | bytes 14000000 | tf_op jit(solution)/shard_map/pallas_call | solution.py:245
  170.7 16.0 %all_to_all.15 = f32[32,16,128]{2,1,0:T(8,128)S(1)} all-to-all(f32[32,16,128]{2,1,0:T(8,128)S(1)} %bitcast.36), channel_id=1, replica_groups=mesh['zh'=2,'x'=4,'core'=2,'y'=4,'zl'=8] {'x','core','y'}, dimensions={0} | all-to-all | bytes 524288 | tf_op jit(solution)/shard_map/all_to_all | solution.py:292
  186.8 20.2 %all_to_all.16 = f32[16,16,128]{2,1,0:T(8,128)S(1)} all-to-all(f32[16,16,128]{2,1,0:T(8,128)S(1)} %broadcast_in_dim.4), channel_id=1, replica_groups=mesh['zh'=2,'x'=4,'core'=2,'y'=4,'zl'=8] {'zh','zl'}, dimensions={0} | all-to-all | bytes 262144 | tf_op jit(solution)/shard_map/all_to_all | solution.py:294
  207.0 15.4 %all_to_all.17 = f32[32,16,128]{2,1,0:T(8,128)S(1)} all-to-all(f32[32,16,128]{2,1,0:T(8,128)S(1)} %broadcast_in_dim.5), channel_id=1, replica_groups=mesh['zh'=2,'x'=4,'core'=2,'y'=4,'zl'=8] {'x','core','y'}, dimensions={0} | all-to-all | bytes 524288 | tf_op jit(solution)/shard_map/all_to_all | solution.py:296
  (54 shorter events, 19.3 us)
Async XLA Ops:
  0.6 74.3 %copy-start = (bf16[96,3072]{1,0:T(8,128)(2,1)S(1)}, bf16[96,3072]{1,0:T(8,128)(2,1)}, u32[]{:S(2)}) copy-start(bf16[96,3072]{1,0:T(8,128)(2,1)} %own0.1) | copy-start | bytes 1769476
  1.6 20.3 %collective-permute-start.6 = (bf16[96,768]{1,0:T(8,128)(2,1)S(1)}, bf16[96,768]{1,0:T(8,128)(2,1)S(1)}, u32[]{:S(2)}, u32[]{:S(2)}) collective-permute-start(bf16[96,768]{1,0:T(8,128)(2,1)S(1)} %constant_dynamic-slice_fusion), channel_id=1, source_target_pairs={{0,256},{256,0},{1,257},{257,1},{2,258},{258,2},{3,259},{259,3},{4... | collective-permute-start | bytes 442376 | tf_op jit(solution)/shard_map/ppermute | solution.py:280
  21.9 16.1 %collective-permute-start.7 = (bf16[96,768]{1,0:T(8,128)(2,1)S(1)}, bf16[96,768]{1,0:T(8,128)(2,1)S(1)}, u32[]{:S(2)}, u32[]{:S(2)}) collective-permute-start(bf16[96,768]{1,0:T(8,128)(2,1)S(1)} %collective-permute-done.6), channel_id=1, source_target_pairs={{0,64},{64,128},{128,192},{192,0},{1,65},{65,129},{129,193},{193,1... | collective-permute-start | bytes 442376 | tf_op jit(solution)/shard_map/ppermute | solution.py:281
  24.6 47.3 %collective-permute-start.2 = (bf16[96,3072]{1,0:T(8,128)(2,1)}, bf16[96,3072]{1,0:T(8,128)(2,1)S(1)}, u32[]{:S(2)}, u32[]{:S(2)}) collective-permute-start(bf16[96,3072]{1,0:T(8,128)(2,1)} %own0.1), channel_id=1, source_target_pairs={{0,64},{64,128},{128,192},{192,0},{1,65},{65,129},{129,193},{193,1... | collective-permute-start | bytes 1769480 | tf_op jit(solution)/shard_map/ppermute | solution.py:284
  27.7 47.1 %collective-permute-start.3 = (bf16[96,3072]{1,0:T(8,128)(2,1)}, bf16[96,3072]{1,0:T(8,128)(2,1)S(1)}, u32[]{:S(2)}, u32[]{:S(2)}) collective-permute-start(bf16[96,3072]{1,0:T(8,128)(2,1)} %own0.1), channel_id=1, source_target_pairs={{0,128},{64,192},{128,0},{192,64},{1,129},{65,193},{129,1},{193,65... | collective-permute-start | bytes 1769480 | tf_op jit(solution)/shard_map/ppermute | solution.py:284
  31.5 43.4 %collective-permute-start.4 = (bf16[96,3072]{1,0:T(8,128)(2,1)}, bf16[96,3072]{1,0:T(8,128)(2,1)S(1)}, u32[]{:S(2)}, u32[]{:S(2)}) collective-permute-start(bf16[96,3072]{1,0:T(8,128)(2,1)} %own0.1), channel_id=1, source_target_pairs={{0,192},{64,0},{128,64},{192,128},{1,193},{65,1},{129,65},{193,129... | collective-permute-start | bytes 1769480 | tf_op jit(solution)/shard_map/ppermute | solution.py:284
  34.9 22.8 %collective-permute-start.8 = (bf16[96,768]{1,0:T(8,128)(2,1)S(1)}, bf16[96,768]{1,0:T(8,128)(2,1)S(1)}, u32[]{:S(2)}, u32[]{:S(2)}) collective-permute-start(bf16[96,768]{1,0:T(8,128)(2,1)S(1)} %collective-permute-done.6), channel_id=1, source_target_pairs={{0,128},{64,192},{128,0},{192,64},{1,129},{65,193},{129,1},{193,65... | collective-permute-start | bytes 442376 | tf_op jit(solution)/shard_map/ppermute | solution.py:281
  38.0 25.5 %collective-permute-start.9 = (bf16[96,768]{1,0:T(8,128)(2,1)S(1)}, bf16[96,768]{1,0:T(8,128)(2,1)S(1)}, u32[]{:S(2)}, u32[]{:S(2)}) collective-permute-start(bf16[96,768]{1,0:T(8,128)(2,1)S(1)} %collective-permute-done.6), channel_id=1, source_target_pairs={{0,192},{64,0},{128,64},{192,128},{1,193},{65,1},{129,65},{193,129... | collective-permute-start | bytes 442376 | tf_op jit(solution)/shard_map/ppermute | solution.py:281
  64.1 12.3 %copy-start.3 = (bf16[384,768]{1,0:T(8,128)(2,1)}, bf16[384,768]{1,0:T(8,128)(2,1)S(1)}, u32[]{:S(2)}) copy-start(bf16[384,768]{1,0:T(8,128)(2,1)S(1)} %get-tuple-element.22.ya0) | copy-start | bytes 1769476
  64.1 17.0 %collective-permute-start.10 = (bf16[384,768]{1,0:T(8,128)(2,1)S(1)}, bf16[384,768]{1,0:T(8,128)(2,1)S(1)}, u32[]{:S(2)}, u32[]{:S(2)}) collective-permute-start(bf16[384,768]{1,0:T(8,128)(2,1)S(1)} %get-tuple-element.22.ya0), channel_id=1, source_target_pairs={{0,8},{8,16},{16,24},{24,0},{1,9},{9,17},{17,25},{25,1},{2,10},{10... | collective-permute-start | bytes 1769480 | tf_op jit(solution)/shard_map/ppermute | solution.py:283
  67.3 26.8 %collective-permute-start.11 = (bf16[384,768]{1,0:T(8,128)(2,1)S(1)}, bf16[384,768]{1,0:T(8,128)(2,1)S(1)}, u32[]{:S(2)}, u32[]{:S(2)}) collective-permute-start(bf16[384,768]{1,0:T(8,128)(2,1)S(1)} %get-tuple-element.22.ya0), channel_id=1, source_target_pairs={{0,16},{8,24},{16,0},{24,8},{1,17},{9,25},{17,1},{25,9},{2,18},{10... | collective-permute-start | bytes 1769480 | tf_op jit(solution)/shard_map/ppermute | solution.py:283
  71.9 24.8 %collective-permute-start.12 = (bf16[384,768]{1,0:T(8,128)(2,1)S(1)}, bf16[384,768]{1,0:T(8,128)(2,1)S(1)}, u32[]{:S(2)}, u32[]{:S(2)}) collective-permute-start(bf16[384,768]{1,0:T(8,128)(2,1)S(1)} %get-tuple-element.22.ya0), channel_id=1, source_target_pairs={{0,24},{8,0},{16,8},{24,16},{1,25},{9,1},{17,9},{25,17},{2,26},{10... | collective-permute-start | bytes 1769480 | tf_op jit(solution)/shard_map/ppermute | solution.py:283
  76.5 26.2 %copy-start.7 = (bf16[1,256,1536]{2,1,0:T(8,128)(2,1)S(1)}, bf16[1,256,1536]{2,1,0:T(8,128)(2,1)}, u32[]{:S(2)}) copy-start(bf16[1,256,1536]{2,1,0:T(8,128)(2,1)} %param.8) | copy-start | bytes 2359300
  76.5 61.5 %collective-permute-start.5 = (bf16[384,3072]{1,0:T(8,128)(2,1)}, bf16[384,3072]{1,0:T(8,128)(2,1)}, u32[]{:S(2)}, u32[]{:S(2)}) collective-permute-start(bf16[384,3072]{1,0:T(8,128)(2,1)} %pad_maximum_fusion), channel_id=1, source_target_pairs={{0,32},{32,0},{1,33},{33,1},{2,34},{34,2},{3,35},{35,3},{4,36},{36... | collective-permute-start | bytes 7077896 | tf_op jit(solution)/shard_map/ppermute | solution.py:285
  82.0 35.9 %copy-start.9 = (s32[1,64]{1,0:T(1,128)S(1)}, s32[1,64]{1,0:T(1,128)}, u32[]{:S(2)}) copy-start(s32[1,64]{1,0:T(1,128)} %param.10) | copy-start | bytes 772
  82.0 36.6 %copy-start.8 = (f32[1536]{0:T(1024)S(1)}, f32[1536]{0:T(1024)}, u32[]{:S(2)}) copy-start(f32[1536]{0:T(1024)} %param.11) | copy-start | bytes 18436
  97.5 0.8 copy-start.1
  98.4 39.6 %collective-permute-start.13 = (bf16[1536,768]{1,0:T(8,128)(2,1)}, bf16[1536,768]{1,0:T(8,128)(2,1)}, u32[]{:S(2)}, u32[]{:S(2)}) collective-permute-start(bf16[1536,768]{1,0:T(8,128)(2,1)} %constant_dynamic-update-slice_fusion.4), channel_id=1, source_target_pairs={{0,32},{32,0},{1,33},{33,1},{2,34},{34,2},{3,35},{35,3},{4,36},{36... | collective-permute-start | bytes 7077896 | tf_op jit(solution)/shard_map/ppermute | solution.py:286
  103.5 19.4 %collective-permute-start.1 = (bf16[96,1536]{1,0:T(8,128)(2,1)}, bf16[96,1536]{1,0:T(8,128)(2,1)}, u32[]{:S(2)}, u32[]{:S(2)}) collective-permute-start(bf16[96,1536]{1,0:T(8,128)(2,1)} %pad_maximum_fusion.2), channel_id=1, source_target_pairs={{0,31},{1,0},{2,1},{3,2},{4,3},{5,4},{6,5},{7,6},{8,7},{9,8},{10,9... | collective-permute-start | bytes 884744 | tf_op jit(solution)/shard_map/ppermute | solution.py:314
  112.3 25.6 %collective-permute-start = (bf16[96,1536]{1,0:T(8,128)(2,1)}, bf16[96,1536]{1,0:T(8,128)(2,1)}, u32[]{:S(2)}, u32[]{:S(2)}) collective-permute-start(bf16[96,1536]{1,0:T(8,128)(2,1)} %pad_maximum_fusion.1), channel_id=1, source_target_pairs={{0,1},{1,2},{2,3},{3,4},{4,5},{5,6},{6,7},{7,8},{8,9},{9,10},{10,1... | collective-permute-start | bytes 884744 | tf_op jit(solution)/shard_map/ppermute | solution.py:313
  138.0 1.1 copy-start.2
  139.1 1.1 copy-start.4
  140.1 0.6 copy-start.5
  140.7 0.9 copy-start.6

commit v2 on v1

--- a/solution.py
+++ b/solution.py
@@ -13,6 +13,7 @@
 HG = 16
 EXG = BLK + 2 * HG
 SHARD = 96
+HALF = 768
 QUART = 768
 LT = D // 128
 SLOT = 40
@@ -30,13 +31,12 @@
     return [(i, (i + by) % count) for i in range(count)]
 
 
-def fused(sc, x_hbm, og_hbm, hp, hn, gain, bias, dw, own0, own1, own2, own3, oc,
-          ya0, ya1, ya2, ya3, yb,
+def fused(sc, x_hbm, og_hbm, hp, hn, dw, near, ya0, ya1, ya2, ya3, yb0, yb1, yb2, yb3,
           act_ref, ig_ref, red_ref,
           xe, oge, w, nrm, std, inv, gbuf, abuf, sbuf, slp, wb, kacc, gh, gn,
           xsem, wsem):
     pos, length = sc[0], sc[1]
-    zh, xi, ci, yi = sc[2], sc[3], sc[4], sc[5]
+    zh, ci, turn = sc[2], sc[3], sc[4]
 
     xcopies = []
 
@@ -61,26 +61,21 @@
     def row_of(z, x, c):
         return pl.multiple_of((z * 8 + x * 2 + c) * SHARD, SHARD)
 
+    go(near, w.at[pl.ds(pl.multiple_of(zh * HALF, HALF), HALF)], wsem.at[32], wcopies)
     k = 0
-    for r, ref in enumerate((own0, own1, own2, own3)):
-        xr = lax.rem(xi + 4 - r, 4)
-        go(ref, w.at[pl.ds(row_of(zh, xr, ci), SHARD)], wsem.at[k], wcopies)
-        go(oc.at[pl.ds(r * SHARD, SHARD)], w.at[pl.ds(row_of(zh, xr, 1 - ci), SHARD)], wsem.at[k + 1], wcopies)
-        k += 2
-    for dy, ref in enumerate((ya0, ya1, ya2, ya3)):
-        col = pl.multiple_of(lax.rem(yi + 4 - dy, 4) * QUART, QUART)
+    for d, (ra, rb) in enumerate(((ya0, yb0), (ya1, yb1), (ya2, yb2), (ya3, yb3))):
+        col = pl.multiple_of(lax.rem(turn + 4 - d, 4) * QUART, QUART)
         for r in range(4):
-            xr = lax.rem(xi + 4 - r, 4)
-            go(ref.at[pl.ds(r * SHARD, SHARD)], w.at[pl.ds(row_of(1 - zh, xr, ci), SHARD), pl.ds(col, QUART)], wsem.at[k], wcopies)
-            go(yb.at[pl.ds((dy * 4 + r) * SHARD, SHARD)], w.at[pl.ds(row_of(1 - zh, xr, 1 - ci), SHARD), pl.ds(col, QUART)], wsem.at[k + 1], wcopies)
+            go(ra.at[pl.ds(r * SHARD, SHARD)], w.at[pl.ds(row_of(1 - zh, r, ci), SHARD), pl.ds(col, QUART)], wsem.at[k], wcopies)
+            go(rb.at[pl.ds(r * SHARD, SHARD)], w.at[pl.ds(row_of(1 - zh, r, 1 - ci), SHARD), pl.ds(col, QUART)], wsem.at[k + 1], wcopies)
             k += 2
 
     red_ref[...] = jnp.zeros((PACK, 128), F32)
     for c in xcopies:
         c.wait()
 
-    gain_row = gain[...]
-    bias_row = bias[...]
+    gain_row = dw[TAPS:TAPS + 1, :]
+    bias_row = dw[TAPS + 1:TAPS + 2, :]
 
     def norm_step(i, carry):
         rows = pl.ds(pl.multiple_of(i * 32, 32), 32)
@@ -239,8 +234,8 @@
         red_ref[l * SLOT + TAPS + 1:l * SLOT + TAPS + 2, :] = brow[:, l * 128:(l + 1) * 128]
 
 
-def run_fused(scalars, frames, out_grad, hp, hn, gain, bias, dw, pieces):
-    any_spec = pl.BlockSpec(memory_space=pl.ANY)
+def run_fused(scalars, frames, out_grad, hp, hn, params, pieces):
+    any_spec = pl.BlockSpec(memory_space=pltpu.HBM)
     vm = pl.BlockSpec(memory_space=pltpu.VMEM)
     return pl.pallas_call(
         fused,
@@ -249,7 +244,7 @@
             jax.ShapeDtypeStruct((2 * BLK, D), BF16),
             jax.ShapeDtypeStruct((PACK, 128), F32),
         ),
-        in_specs=[pl.BlockSpec(memory_space=pltpu.SMEM)] + [any_spec] * 4 + [vm] * 3 + [any_spec] * len(pieces),
+        in_specs=[pl.BlockSpec(memory_space=pltpu.SMEM)] + [any_spec] * 4 + [vm] + [any_spec] * len(pieces),
         out_specs=(vm, vm, vm),
         scratch_shapes=[
             pltpu.VMEM((2 * EXT, D), BF16),
@@ -271,20 +266,75 @@
         ],
         compiler_params=pltpu.CompilerParams(vmem_limit_bytes=48 * 1024 * 1024),
         cost_estimate=pl.CostEstimate(flops=9_000_000_000, bytes_accessed=14_000_000, transcendentals=2_000_000),
-    )(scalars, frames, out_grad, hp, hn, gain, bias, dw, *pieces)
-
-
-def gather_weight(own):
-    yi = lax.axis_index("y")
-    quarter = lax.dynamic_slice_in_dim(own, yi * QUART, QUART, axis=1)
-    far = lax.ppermute(quarter, "zh", shift(2, 1))
-    far = [far] + [lax.ppermute(far, "x", shift(4, d)) for d in (1, 2, 3)]
-    far = jnp.concatenate(far, axis=0)
-    ya = [far] + [lax.ppermute(far, "y", shift(4, d)) for d in (1, 2, 3)]
-    mine = [own] + [lax.ppermute(own, "x", shift(4, d)) for d in (1, 2, 3)]
-    oc = lax.ppermute(jnp.concatenate(mine, axis=0), "core", shift(2, 1))
-    yb = lax.ppermute(jnp.concatenate(ya, axis=0), "core", shift(2, 1))
-    return mine + [oc] + ya + [yb]
+    )(scalars, frames, out_grad, hp, hn, params, *pieces)
+
+
+def take_rims(x, g, tails, heads, sem):
+    copies = []
+    for dst, fx, fg in ((tails, BLK - HX, BLK - HG), (heads, 0, 0)):
+        for s in range(2):
+            copies.append(pltpu.make_async_copy(x.at[pl.ds(s * BLK + fx, HX)], dst.at[pl.ds(s * HX, HX)], sem.at[len(copies)]))
+            copies.append(pltpu.make_async_copy(g.at[pl.ds(s * BLK + fg, HG)], dst.at[pl.ds(2 * HX + s * HG, HG)], sem.at[len(copies)]))
+    for c in copies:
+        c.start()
+    for c in copies:
+        c.wait()
+
+
+def rims(x, g):
+    any_spec = pl.BlockSpec(memory_space=pltpu.HBM)
+    shape = jax.ShapeDtypeStruct((2 * (HX + HG), D), BF16)
+    return pl.pallas_call(
+        take_rims,
+        out_shape=(shape, shape),
+        in_specs=[any_spec] * 2,
+        out_specs=(any_spec, any_spec),
+        scratch_shapes=[pltpu.SemaphoreType.DMA((8,))],
+        compiler_params=pltpu.CompilerParams(vmem_limit_bytes=1024 * 1024),
+        cost_estimate=pl.CostEstimate(flops=0, bytes_accessed=30_000_000, transcendentals=0),
+    )(x, g)
+
+
+def write_copies(src, dst, sem):
+    copies = [pltpu.make_async_copy(src, dst.at[i], sem.at[i]) for i in range(4)]
+    for c in copies:
+        c.start()
+    for c in copies:
+        c.wait()
+
+
+def four_copies(part):
+    any_spec = pl.BlockSpec(memory_space=pltpu.HBM)
+    return pl.pallas_call(
+        write_copies,
+        out_shape=jax.ShapeDtypeStruct((4,) + part.shape, part.dtype),
+        in_specs=[any_spec],
+        out_specs=any_spec,
+        scratch_shapes=[pltpu.SemaphoreType.DMA((4,))],
+        compiler_params=pltpu.CompilerParams(vmem_limit_bytes=1024 * 1024),
+        cost_estimate=pl.CostEstimate(flops=0, bytes_accessed=1_200_000, transcendentals=0),
+    )(part)
+
+
+def gather_weight(own, turn, tails, heads, params):
+    theirs = lax.rem(turn + 2, 4)
+    quarter = lax.dynamic_slice_in_dim(own, theirs * QUART, QUART, axis=1)
+    near = lax.all_gather(own, ("x", "core"), axis=0, tiled=True)
+    far = lax.ppermute(quarter, ("zh", "zl"), [(i, 15 - i) for i in range(16)])
+    far = four_copies(far)
+    hp = lax.ppermute(tails, ("y", "zl"), shift(32, 1))
+    hn = lax.ppermute(heads, ("y", "zl"), shift(32, -1))
+    far = lax.all_to_all(far, "x", 0, 0)
+    far, hp, hn, params = lax.optimization_barrier((far, hp, hn, params))
+    far = far.reshape(4 * SHARD, QUART)
+    ya = [
+        far,
+        lax.ppermute(far, "y", shift(4, 1)),
+        lax.ppermute(far, "zl", [(i, i ^ 1) for i in range(8)]),
+        lax.ppermute(far, "y", shift(4, -1)),
+    ]
+    yb = [lax.ppermute(part, "core", shift(2, 1)) for part in ya]
+    return hp, hn, params, [near] + ya + yb
 
 
 def reduce_all(packed):
@@ -305,15 +355,14 @@
     dy = out_grad.reshape(2 * BLK, D)
     seq = idx("y") * 8 + idx("zl")
     position = jnp.mod(seq - owner_map[0, 0], 32)
-    scalars = jnp.stack([position, lengths[0], idx("zh"), idx("x"), idx("core"), idx("y"), position, position]).astype(jnp.int32)
-
-    tails = jnp.concatenate([x[BLK - HX:BLK], x[2 * BLK - HX:], dy[BLK - HG:BLK], dy[2 * BLK - HG:]], axis=0)
-    heads = jnp.concatenate([x[:HX], x[BLK:BLK + HX], dy[:HG], dy[BLK:BLK + HG]], axis=0)
-    pieces = gather_weight(proj_weight)
-    hp = lax.ppermute(tails, ("y", "zl"), shift(32, 1))
-    hn = lax.ppermute(heads, ("y", "zl"), shift(32, -1))
+    turn = lax.rem(idx("y") + 2 * lax.rem(idx("zl"), 2), 4)
+    scalars = jnp.stack([position, lengths[0], idx("zh"), idx("core"), turn, position, position, position]).astype(jnp.int32)
+
+    tails, heads = rims(x, dy)
+    params = jnp.concatenate([dw_kernel, norm_gain[None], norm_bias[None]], axis=0)
+    hp, hn, params, pieces = gather_weight(proj_weight, turn, tails, heads, params)
     act, ig, packed = run_fused(
-        scalars, x, dy, hp, hn, norm_gain.reshape(1, D), norm_bias.reshape(1, D), dw_kernel, pieces)
+        scalars, x, dy, hp, hn, params, pieces)
     kernel_grad, gain_grad, bias_grad = reduce_all(packed)
     return act.reshape(1, 2 * BLK, D), ig.reshape(1, 2 * BLK, D), kernel_grad, gain_grad, bias_grad
 

time: 225 us -> 181 us (0.80)
  waiting for transfers between devices: 56.1 us -> 18.7 us
  between operations: 1.63 us -> 15 us
  starting transfers between devices: 67.8 us -> 54.8 us
  local copies, waits for them, and re-layouts: 14.6 us -> 7.99 us
    ppermute x14 -> x10, waiting for transfers between devices: 56.1 us -> 18 us  [the longest x1 13.4 us: gather_weight(): far = lax.ppermute(quarter, ('zh', 'zl'), [(i, 15 - i) for i in range(16)])]
    ppermute x14 -> x10, starting transfers between devices: 67.8 us -> 50.7 us  [the longest x4 17.5 us: gather_weight(): yb = [lax.ppermute(part, 'core', shift(2, 1)) for part in ya]]
    unnamed x28 -> x12, local copies, waits for them, and re-layouts: 9.71 us -> 4.77 us
    all_to_all x0 -> x1, starting transfers between devices: none -> 4.02 us  [gather_weight(): far = lax.all_to_all(far, 'x', 0, 0)]
    all_to_all x1, blocking collectives: 20.2 us -> 22.9 us  [reduce_all(): lax.all_to_all(jnp.broadcast_to(mine[None], (16,) + mine.shape), ('zh', '...]
    all_to_all x1, blocking collectives: 16 us -> 13.6 us  [reduce_all(): parts = lax.all_to_all(packed.reshape(32, PACK // 32, 128), plane, 0, 0)]
  transfers between devices with their start and end apart: 14 -> 12, of which waited for: 7 -> 5; matrix products, arithmetic and copies ran while one was open for 5% -> 2% of each run, Pallas kernels for 0% -> 1%
where the time goes in v2:
time: 181 us; the launch traced here: 180 us
  starting transfers between devices  54.8 us (30%)
  blocking collectives  51.9 us (29%)
  Pallas kernels  30.9 us (17%)
  waiting for transfers between devices  18.7 us (10%)
  between operations  15 us (8%)
  local copies, waits for them, and re-layouts  7.99 us (4%)
    pallas_call x1, Pallas kernels, run_fused(): pl.pallas_call(fused, out_shape=(jax.ShapeDtypeStruct((2 * BLK, D), BF16)...  29.3 us
    all_to_all x1, blocking collectives, reduce_all(): lax.all_to_all(jnp.broadcast_to(mine[None], (16,) + mine.shape), ('zh', '...  22.9 us
    ppermute x4, starting transfers between devices, gather_weight(): yb = [lax.ppermute(part, 'core', shift(2, 1)) for part in ya]  17.5 us
    all_to_all x1, blocking collectives, reduce_all(): lax.all_to_all(jnp.broadcast_to(mine[None], (32,) + mine.shape), plane, 0...  15.4 us
    all_to_all x1, blocking collectives, reduce_all(): parts = lax.all_to_all(packed.reshape(32, PACK // 32, 128), plane, 0, 0)  13.6 us
    ppermute x1, waiting for transfers between devices, gather_weight(): far = lax.ppermute(quarter, ('zh', 'zl'), [(i, 15 - i) for i in range(16)])  13.4 us
    ppermute x1, starting transfers between devices, gather_weight(): hn = lax.ppermute(heads, ('y', 'zl'), shift(32, -1))  12.1 us
    ppermute x1, starting transfers between devices, gather_weight(): far = lax.ppermute(quarter, ('zh', 'zl'), [(i, 15 - i) for i in range(16)])  12 us
  transfers between devices with their start and end apart: 12, of which 5 were waited for; matrix products, arithmetic and copies ran while one was open for 2% of the time, Pallas kernels for 1%

profile of v2, /device:TPU:1, one launch (start us, length us, event | category | flops | bytes accessed | tf_op | source)
XLA Modules:
  0.0 180.2 jit_solution(13836079608239625407)
XLA Ops:
  7.9 0.9 constant_dynamic-slice_fusion
  8.9 12.0 %collective-permute-start = (bf16[96,768]{1,0:T(8,128)(2,1)S(1)}, bf16[96,768]{1,0:T(8,128)(2,1)S(1)}, u32[]{:S(2)}, u32[]{:S(2)}) collective-permute-start(bf16[96,768]{1,0:T(8,128)(2,1)S(1)} %constant_dynamic-slice_fusion), channel_id=1, source_target_pairs={{0,263},{1,262},{2,261},{3,260},{4,259},{5,258},{6,257},{7,256},{2... | collective-permute-start | bytes 442376 | tf_op jit(solution)/shard_map/ppermute | solution.py:323
  20.8 13.4 %collective-permute-done.src = bf16[96,768]{1,0:T(8,128)(2,1)S(1)} collective-permute-done((bf16[96,768]{1,0:T(8,128)(2,1)S(1)}, bf16[96,768]{1,0:T(8,128)(2,1)S(1)}, u32[]{:S(2)}, u32[]{:S(2)}) %collective-permute-start) | collective-permute-done | bytes 147488 | tf_op jit(solution)/shard_map/ppermute | solution.py:323
  35.0 4.0 %all-to-all-start = ((bf16[4,96,768]{2,1,0:T(8,128)(2,1)}), bf16[4,96,768]{2,1,0:T(8,128)(2,1)S(1)}, u32[]{:S(2)}, u32[]{:S(2)}) async-start(bf16[4,96,768]{2,1,0:T(8,128)(2,1)} %shard_map.119), calls=%async_computation | async-start | bytes 1179648 | tf_op jit(solution)/shard_map/all_to_all | solution.py:327
  39.1 1.1 copy-done
  40.2 1.2 copy-done.1
  42.2 1.9 %collective-permute-start.1 = (bf16[96,1536]{1,0:T(8,128)(2,1)S(1)}, bf16[96,1536]{1,0:T(8,128)(2,1)S(1)}, u32[]{:S(2)}, u32[]{:S(2)}) collective-permute-start(bf16[96,1536]{1,0:T(8,128)(2,1)S(1)} %get-tuple-element.14), channel_id=1, source_target_pairs={{0,1},{1,2},{2,3},{3,4},{4,5},{5,6},{6,7},{7,8},{8,9},{9,10},{10,1... | collective-permute-start | bytes 884744 | tf_op jit(solution)/shard_map/ppermute | solution.py:325
  44.1 12.1 %collective-permute-start.2 = (bf16[96,1536]{1,0:T(8,128)(2,1)S(1)}, bf16[96,1536]{1,0:T(8,128)(2,1)S(1)}, u32[]{:S(2)}, u32[]{:S(2)}) collective-permute-start(bf16[96,1536]{1,0:T(8,128)(2,1)S(1)} %get-tuple-element.15), channel_id=1, source_target_pairs={{0,31},{1,0},{2,1},{3,2},{4,3},{5,4},{6,5},{7,6},{8,7},{9,8},{10,9... | collective-permute-start | bytes 884744 | tf_op jit(solution)/shard_map/ppermute | solution.py:326
  57.6 1.0 pad_maximum_fusion.dw
  58.6 1.7 collective-permute-done.1.hp
  61.8 3.4 %collective-permute-start.5 = (bf16[384,768]{1,0:T(8,128)(2,1)S(1)}, bf16[384,768]{1,0:T(8,128)(2,1)S(1)}, u32[]{:S(2)}, u32[]{:S(2)}) collective-permute-start(bf16[384,768]{1,0:T(8,128)(2,1)S(1)} %bitcast.24), channel_id=1, source_target_pairs={{0,24},{8,0},{16,8},{24,16},{1,25},{9,1},{17,9},{25,17},{2,26},{10... | collective-permute-start | bytes 1769480 | tf_op jit(solution)/shard_map/ppermute | solution.py:334
  65.2 1.9 %collective-permute-start.4 = (bf16[384,768]{1,0:T(8,128)(2,1)S(1)}, bf16[384,768]{1,0:T(8,128)(2,1)S(1)}, u32[]{:S(2)}, u32[]{:S(2)}) collective-permute-start(bf16[384,768]{1,0:T(8,128)(2,1)S(1)} %bitcast.25), channel_id=1, source_target_pairs={{0,1},{1,0},{2,3},{3,2},{4,5},{5,4},{6,7},{7,6},{8,9},{9,8},{10,11... | collective-permute-start | bytes 1769480 | tf_op jit(solution)/shard_map/ppermute | solution.py:333
  67.1 1.9 %collective-permute-start.3 = (bf16[384,768]{1,0:T(8,128)(2,1)S(1)}, bf16[384,768]{1,0:T(8,128)(2,1)S(1)}, u32[]{:S(2)}, u32[]{:S(2)}) collective-permute-start(bf16[384,768]{1,0:T(8,128)(2,1)S(1)} %bitcast.26), channel_id=1, source_target_pairs={{0,8},{8,16},{16,24},{24,0},{1,9},{9,17},{17,25},{25,1},{2,10},{10... | collective-permute-start | bytes 1769480 | tf_op jit(solution)/shard_map/ppermute | solution.py:332
  69.0 5.3 %collective-permute-start.6 = (bf16[384,768]{1,0:T(8,128)(2,1)S(1)}, bf16[384,768]{1,0:T(8,128)(2,1)S(1)}, u32[]{:S(2)}, u32[]{:S(2)}) collective-permute-start(bf16[384,768]{1,0:T(8,128)(2,1)S(1)} %bitcast.27), channel_id=1, source_target_pairs={{0,32},{32,0},{1,33},{33,1},{2,34},{34,2},{3,35},{35,3},{4,36},{36... | collective-permute-start | bytes 1769480 | tf_op jit(solution)/shard_map/ppermute | solution.py:336
  74.3 1.3 collective-permute-done.5.ya3
  75.6 5.7 %collective-permute-start.9 = (bf16[384,768]{1,0:T(8,128)(2,1)S(1)}, bf16[384,768]{1,0:T(8,128)(2,1)}, u32[]{:S(2)}, u32[]{:S(2)}) collective-permute-start(bf16[384,768]{1,0:T(8,128)(2,1)S(1)} %collective-permute-done.5.ya3), channel_id=1, source_target_pairs={{0,32},{32,0},{1,33},{33,1},{2,34},{34,2},{3,35},{35,3},{4,36},{36... | collective-permute-start | bytes 1769480 | tf_op jit(solution)/shard_map/ppermute | solution.py:336
  81.3 3.4 %collective-permute-start.8 = (bf16[384,768]{1,0:T(8,128)(2,1)S(1)}, bf16[384,768]{1,0:T(8,128)(2,1)}, u32[]{:S(2)}, u32[]{:S(2)}) collective-permute-start(bf16[384,768]{1,0:T(8,128)(2,1)S(1)} %collective-permute-done.4.ya2), channel_id=1, source_target_pairs={{0,32},{32,0},{1,33},{33,1},{2,34},{34,2},{3,35},{35,3},{4,36},{36... | collective-permute-start | bytes 1769480 | tf_op jit(solution)/shard_map/ppermute | solution.py:336
  84.7 3.1 %collective-permute-start.7 = (bf16[384,768]{1,0:T(8,128)(2,1)S(1)}, bf16[384,768]{1,0:T(8,128)(2,1)}, u32[]{:S(2)}, u32[]{:S(2)}) collective-permute-start(bf16[384,768]{1,0:T(8,128)(2,1)S(1)} %collective-permute-done.3.ya1), channel_id=1, source_target_pairs={{0,32},{32,0},{1,33},{33,1},{2,34},{34,2},{3,35},{35,3},{4,36},{36... | collective-permute-start | bytes 1769480 | tf_op jit(solution)/shard_map/ppermute | solution.py:336
  88.7 0.9 collective-permute-done.7.yb1
  89.6 1.0 copy-done.3
  90.6 29.3 %shard_map.121 = (bf16[256,1536]{1,0:T(8,128)(2,1)}, bf16[256,1536]{1,0:T(8,128)(2,1)}, f32[512,128]{1,0:T(8,128)S(1)}) custom-call(s32[8]{0:T(128)S(1)} %stack.22.sc, bf16[256,1536]{1,0:T(8,128)(2,1)} %bitcast.20, bf16[256,1536]{1,0:T(8,128)(2,1)} %bitcast.22, bf16[96,1536]{1,0:T(8,128)(2,1)S(1)} %collective-permute-done.1.hp, ...), custom_call_target="tpu_custom_call" | custom-call | flops 8999999488 | bytes 14000000 | tf_op jit(solution)/shard_map/pallas_call | solution.py:240
  119.8 13.6 %all_to_all.20 = f32[32,16,128]{2,1,0:T(8,128)S(1)} all-to-all(f32[32,16,128]{2,1,0:T(8,128)S(1)} %bitcast.29), channel_id=1, replica_groups=mesh['zh'=2,'x'=4,'core'=2,'y'=4,'zl'=8] {'x','core','y'}, dimensions={0} | all-to-all | bytes 524288 | tf_op jit(solution)/shard_map/all_to_all | solution.py:342
  133.5 22.9 %all_to_all.21 = f32[16,16,128]{2,1,0:T(8,128)S(1)} all-to-all(f32[16,16,128]{2,1,0:T(8,128)S(1)} %broadcast_in_dim.20), channel_id=1, replica_groups=mesh['zh'=2,'x'=4,'core'=2,'y'=4,'zl'=8] {'zh','zl'}, dimensions={0} | all-to-all | bytes 262144 | tf_op jit(solution)/shard_map/all_to_all | solution.py:344
  156.4 15.4 %all_to_all.22 = f32[32,16,128]{2,1,0:T(8,128)S(1)} all-to-all(f32[32,16,128]{2,1,0:T(8,128)S(1)} %broadcast_in_dim.21), channel_id=1, replica_groups=mesh['zh'=2,'x'=4,'core'=2,'y'=4,'zl'=8] {'x','core','y'}, dimensions={0} | all-to-all | bytes 524288 | tf_op jit(solution)/shard_map/all_to_all | solution.py:346
  (32 shorter events, 7.0 us)
Async XLA Ops:
  7.2 80.7 %copy-start.4 = (s32[1,64]{1,0:T(1,128)S(1)}, s32[1,64]{1,0:T(1,128)}, u32[]{:S(2)}) copy-start(s32[1,64]{1,0:T(1,128)} %param.10) | copy-start | bytes 772
  7.2 82.4 %all-gather.2.cloned.1.call-start = ((), (), s32[]{:S(2)}) async-start(), calls=%async_computation.4 | async-start | bytes 5308416 | tf_op jit(solution)/shard_map/all_gather | solution.py:322
  8.9 25.3 %collective-permute-start = (bf16[96,768]{1,0:T(8,128)(2,1)S(1)}, bf16[96,768]{1,0:T(8,128)(2,1)S(1)}, u32[]{:S(2)}, u32[]{:S(2)}) collective-permute-start(bf16[96,768]{1,0:T(8,128)(2,1)S(1)} %constant_dynamic-slice_fusion), channel_id=1, source_target_pairs={{0,263},{1,262},{2,261},{3,260},{4,259},{5,258},{6,257},{7,256},{2... | collective-permute-start | bytes 442376 | tf_op jit(solution)/shard_map/ppermute | solution.py:323
  35.0 26.7 %all-to-all-start = ((bf16[4,96,768]{2,1,0:T(8,128)(2,1)}), bf16[4,96,768]{2,1,0:T(8,128)(2,1)S(1)}, u32[]{:S(2)}, u32[]{:S(2)}) async-start(bf16[4,96,768]{2,1,0:T(8,128)(2,1)} %shard_map.119), calls=%async_computation | async-start | bytes 1179648 | tf_op jit(solution)/shard_map/all_to_all | solution.py:327
  39.1 1.1 copy-start
  40.2 1.2 copy-start.1
  42.2 18.0 %collective-permute-start.1 = (bf16[96,1536]{1,0:T(8,128)(2,1)S(1)}, bf16[96,1536]{1,0:T(8,128)(2,1)S(1)}, u32[]{:S(2)}, u32[]{:S(2)}) collective-permute-start(bf16[96,1536]{1,0:T(8,128)(2,1)S(1)} %get-tuple-element.14), channel_id=1, source_target_pairs={{0,1},{1,2},{2,3},{3,4},{4,5},{5,6},{6,7},{7,8},{8,9},{9,10},{10,1... | collective-permute-start | bytes 884744 | tf_op jit(solution)/shard_map/ppermute | solution.py:325
  44.1 16.9 %collective-permute-start.2 = (bf16[96,1536]{1,0:T(8,128)(2,1)S(1)}, bf16[96,1536]{1,0:T(8,128)(2,1)S(1)}, u32[]{:S(2)}, u32[]{:S(2)}) collective-permute-start(bf16[96,1536]{1,0:T(8,128)(2,1)S(1)} %get-tuple-element.15), channel_id=1, source_target_pairs={{0,31},{1,0},{2,1},{3,2},{4,3},{5,4},{6,5},{7,6},{8,7},{9,8},{10,9... | collective-permute-start | bytes 884744 | tf_op jit(solution)/shard_map/ppermute | solution.py:326
  61.1 0.7 copy-start.2
  61.8 13.8 %collective-permute-start.5 = (bf16[384,768]{1,0:T(8,128)(2,1)S(1)}, bf16[384,768]{1,0:T(8,128)(2,1)S(1)}, u32[]{:S(2)}, u32[]{:S(2)}) collective-permute-start(bf16[384,768]{1,0:T(8,128)(2,1)S(1)} %bitcast.24), channel_id=1, source_target_pairs={{0,24},{8,0},{16,8},{24,16},{1,25},{9,1},{17,9},{25,17},{2,26},{10... | collective-permute-start | bytes 1769480 | tf_op jit(solution)/shard_map/ppermute | solution.py:334
  65.2 16.1 %collective-permute-start.4 = (bf16[384,768]{1,0:T(8,128)(2,1)S(1)}, bf16[384,768]{1,0:T(8,128)(2,1)S(1)}, u32[]{:S(2)}, u32[]{:S(2)}) collective-permute-start(bf16[384,768]{1,0:T(8,128)(2,1)S(1)} %bitcast.25), channel_id=1, source_target_pairs={{0,1},{1,0},{2,3},{3,2},{4,5},{5,4},{6,7},{7,6},{8,9},{9,8},{10,11... | collective-permute-start | bytes 1769480 | tf_op jit(solution)/shard_map/ppermute | solution.py:333
  67.1 17.6 %collective-permute-start.3 = (bf16[384,768]{1,0:T(8,128)(2,1)S(1)}, bf16[384,768]{1,0:T(8,128)(2,1)S(1)}, u32[]{:S(2)}, u32[]{:S(2)}) collective-permute-start(bf16[384,768]{1,0:T(8,128)(2,1)S(1)} %bitcast.26), channel_id=1, source_target_pairs={{0,8},{8,16},{16,24},{24,0},{1,9},{9,17},{17,25},{25,1},{2,10},{10... | collective-permute-start | bytes 1769480 | tf_op jit(solution)/shard_map/ppermute | solution.py:332
  69.0 19.6 %collective-permute-start.6 = (bf16[384,768]{1,0:T(8,128)(2,1)S(1)}, bf16[384,768]{1,0:T(8,128)(2,1)S(1)}, u32[]{:S(2)}, u32[]{:S(2)}) collective-permute-start(bf16[384,768]{1,0:T(8,128)(2,1)S(1)} %bitcast.27), channel_id=1, source_target_pairs={{0,32},{32,0},{1,33},{33,1},{2,34},{34,2},{3,35},{35,3},{4,36},{36... | collective-permute-start | bytes 1769480 | tf_op jit(solution)/shard_map/ppermute | solution.py:336
  75.6 13.1 %collective-permute-start.9 = (bf16[384,768]{1,0:T(8,128)(2,1)S(1)}, bf16[384,768]{1,0:T(8,128)(2,1)}, u32[]{:S(2)}, u32[]{:S(2)}) collective-permute-start(bf16[384,768]{1,0:T(8,128)(2,1)S(1)} %collective-permute-done.5.ya3), channel_id=1, source_target_pairs={{0,32},{32,0},{1,33},{33,1},{2,34},{34,2},{3,35},{35,3},{4,36},{36... | collective-permute-start | bytes 1769480 | tf_op jit(solution)/shard_map/ppermute | solution.py:336
  81.3 7.4 %collective-permute-start.8 = (bf16[384,768]{1,0:T(8,128)(2,1)S(1)}, bf16[384,768]{1,0:T(8,128)(2,1)}, u32[]{:S(2)}, u32[]{:S(2)}) collective-permute-start(bf16[384,768]{1,0:T(8,128)(2,1)S(1)} %collective-permute-done.4.ya2), channel_id=1, source_target_pairs={{0,32},{32,0},{1,33},{33,1},{2,34},{34,2},{3,35},{35,3},{4,36},{36... | collective-permute-start | bytes 1769480 | tf_op jit(solution)/shard_map/ppermute | solution.py:336
  84.7 4.9 %collective-permute-start.7 = (bf16[384,768]{1,0:T(8,128)(2,1)S(1)}, bf16[384,768]{1,0:T(8,128)(2,1)}, u32[]{:S(2)}, u32[]{:S(2)}) collective-permute-start(bf16[384,768]{1,0:T(8,128)(2,1)S(1)} %collective-permute-done.3.ya1), channel_id=1, source_target_pairs={{0,32},{32,0},{1,33},{33,1},{2,34},{34,2},{3,35},{35,3},{4,36},{36... | collective-permute-start | bytes 1769480 | tf_op jit(solution)/shard_map/ppermute | solution.py:336
  89.6 1.0 copy-start.3
Sparse Core Ops, SparseCore 0:
  10.1 53.9 all-gather.1

commit v3 on v2

--- a/solution.py
+++ b/solution.py
@@ -16,8 +16,9 @@
 HALF = 768
 QUART = 768
 LT = D // 128
-SLOT = 40
 PACK = 512
+GAIN_ROW = 384
+BIAS_ROW = 400
 EPS = 1e-05
 F32 = jnp.float32
 BF16 = jnp.bfloat16
@@ -33,7 +34,7 @@
 
 def fused(sc, x_hbm, og_hbm, hp, hn, dw, near, ya0, ya1, ya2, ya3, yb0, yb1, yb2, yb3,
           act_ref, ig_ref, red_ref,
-          xe, oge, w, nrm, std, inv, gbuf, abuf, sbuf, slp, wb, kacc, gh, gn,
+          xe, oge, w, nrm, std, inv, gbuf, abuf, sbuf, slp, kacc, gh, gn,
           xsem, wsem):
     pos, length = sc[0], sc[1]
     zh, ci, turn = sc[2], sc[3], sc[4]
@@ -78,7 +79,7 @@
     bias_row = dw[TAPS + 1:TAPS + 2, :]
 
     def norm_step(i, carry):
-        rows = pl.ds(pl.multiple_of(i * 32, 32), 32)
+        rows = pl.ds(pl.multiple_of(i * 128, 128), 128)
         v = xe[rows, :].astype(F32)
         mean = jnp.sum(v, axis=1, keepdims=True) * (1.0 / D)
         c = v - mean
@@ -86,11 +87,11 @@
         iv = lax.rsqrt(var + EPS)
         st = c * iv
         std[rows, :] = st
-        inv[rows, :] = jnp.broadcast_to(iv, (32, 128))
+        inv[rows, :] = jnp.broadcast_to(iv, (128, 128))
         nrm[rows, :] = (st * gain_row + bias_row).astype(BF16)
         return carry
 
-    lax.fori_loop(0, 2 * EXT // 32, norm_step, 0)
+    lax.fori_loop(0, 2 * EXT // 128, norm_step, 0)
 
     for c in wcopies:
         c.wait()
@@ -124,10 +125,9 @@
             @pl.when(s == 0)
             def _():
                 for k in range(TAPS):
-                    wb[k] = jnp.broadcast_to(dw[pl.ds(k, 1), pl.ds(lane, 128)], (8, 128))
                     kacc[k] = jnp.zeros((8, 128), F32)
 
-            taps = [wb[k] for k in range(TAPS)]
+            taps = [jnp.broadcast_to(dw[k:k + 1, pl.ds(lane, 128)], (8, 128)) for k in range(TAPS)]
             acc = {}
             done = {}
             for o in range(1, 8 * 19 + 32):
@@ -169,7 +169,7 @@
             @pl.when(s == 1)
             def _():
                 for k in range(TAPS):
-                    red_ref[pl.ds((2 * j + h) * SLOT + k, 1), :] = jnp.sum(ks[k], axis=0, keepdims=True)
+                    red_ref[pl.ds((k // 8) * 8 * LT + k % 8 + (2 * j + h) * 8, 1), :] = jnp.sum(ks[k], axis=0, keepdims=True)
 
             acc = {}
             done = {}
@@ -201,21 +201,16 @@
 
     lax.fori_loop(0, D // 256, chan_step, 0)
 
-    def back_step(n, carry):
-        rows = pl.ds(pl.multiple_of(n * 256, 256), 256)
-        gn[:, rows] = lax.dot_general(gh[...], w[rows, :], (((1,), (1,)), ((), ())), preferred_element_type=F32)
-        return carry
-
-    lax.fori_loop(0, D // 256, back_step, 0)
+    gn[...] = lax.dot_general(gh[...], w[...], (((1,), (1,)), ((), ())), preferred_element_type=F32)
 
     def grad_step(i, carry):
         gsum, bsum = carry
-        src = pl.ds(pl.multiple_of(jnp.where(i >= 4, EXT - BLK, 0) + HX + i * 32, 32), 32)
-        dst = pl.ds(pl.multiple_of(i * 32, 32), 32)
+        src = pl.ds(pl.multiple_of(jnp.where(i >= 2, EXT - BLK, 0) + HX + i * 64, 32), 64)
+        dst = pl.ds(pl.multiple_of(i * 64, 64), 64)
         g = gn[dst, :]
         st = std[src, :]
         gs = g * st
-        for q in range(4):
+        for q in range(8):
             gsum = gsum + gs[q * 8:(q + 1) * 8]
             bsum = bsum + g[q * 8:(q + 1) * 8]
         sc_ = g * gain_row
@@ -226,12 +221,12 @@
         return gsum, bsum
 
     zero = jnp.zeros((8, D), F32)
-    gsum, bsum = lax.fori_loop(0, 8, grad_step, (zero, zero))
+    gsum, bsum = lax.fori_loop(0, 4, grad_step, (zero, zero))
     grow = jnp.sum(gsum, axis=0, keepdims=True)
     brow = jnp.sum(bsum, axis=0, keepdims=True)
     for l in range(LT):
-        red_ref[l * SLOT + TAPS:l * SLOT + TAPS + 1, :] = grow[:, l * 128:(l + 1) * 128]
-        red_ref[l * SLOT + TAPS + 1:l * SLOT + TAPS + 2, :] = brow[:, l * 128:(l + 1) * 128]
+        red_ref[GAIN_ROW + l:GAIN_ROW + l + 1, :] = grow[:, l * 128:(l + 1) * 128]
+        red_ref[BIAS_ROW + l:BIAS_ROW + l + 1, :] = brow[:, l * 128:(l + 1) * 128]
 
 
 def run_fused(scalars, frames, out_grad, hp, hn, params, pieces):
@@ -258,7 +253,6 @@
             pltpu.VMEM((2, 2 * EXT, 128), F32),
             pltpu.VMEM((EXG, 128), F32),
             pltpu.VMEM((TAPS, 8, 128), F32),
-            pltpu.VMEM((TAPS, 8, 128), F32),
             pltpu.VMEM((2 * BLK, 2 * D), BF16),
             pltpu.VMEM((2 * BLK, D), F32),
             pltpu.SemaphoreType.DMA((12,)),
@@ -322,10 +316,11 @@
     near = lax.all_gather(own, ("x", "core"), axis=0, tiled=True)
     far = lax.ppermute(quarter, ("zh", "zl"), [(i, 15 - i) for i in range(16)])
     far = four_copies(far)
+    far, tails, heads, params = lax.optimization_barrier((far, tails, heads, params))
     hp = lax.ppermute(tails, ("y", "zl"), shift(32, 1))
     hn = lax.ppermute(heads, ("y", "zl"), shift(32, -1))
     far = lax.all_to_all(far, "x", 0, 0)
-    far, hp, hn, params = lax.optimization_barrier((far, hp, hn, params))
+    far, hp, hn = lax.optimization_barrier((far, hp, hn))
     far = far.reshape(4 * SHARD, QUART)
     ya = [
         far,
@@ -344,9 +339,9 @@
     line = lax.all_to_all(jnp.broadcast_to(mine[None], (16,) + mine.shape), ("zh", "zl"), 0, 0)
     mine = jnp.sum(line, axis=0)
     whole = lax.all_to_all(jnp.broadcast_to(mine[None], (32,) + mine.shape), plane, 0, 0)
-    whole = whole.reshape(PACK, 128)[: LT * SLOT].reshape(LT, SLOT, 128)
-    whole = jnp.swapaxes(whole, 0, 1).reshape(SLOT, D)
-    return whole[:TAPS], whole[TAPS], whole[TAPS + 1]
+    whole = whole.reshape(PACK, 128)
+    taps = whole[:GAIN_ROW].reshape(4, LT, 8, 128).transpose(0, 2, 1, 3).reshape(32, D)[:TAPS]
+    return taps, whole[GAIN_ROW:GAIN_ROW + LT].reshape(D), whole[BIAS_ROW:BIAS_ROW + LT].reshape(D)
 
 
 def on_device(frames, lengths, owner_map, norm_gain, norm_bias, proj_weight, dw_kernel, out_grad):

time: 181 us -> 175 us (0.967)
  waiting for transfers between devices: 18.7 us -> 15.4 us
  Pallas kernels: 30.9 us -> 28.8 us
    ppermute x1, waiting for transfers between devices: 13.4 us -> 7.9 us  [gather_weight(): far = lax.ppermute(quarter, ('zh', 'zl'), [(i, 15 - i) for i in range(16)])]
    ppermute x1, waiting for transfers between devices: 1.66 us -> 3.99 us  [gather_weight(): hp = lax.ppermute(tails, ('y', 'zl'), shift(32, 1))]
    pallas_call x1, Pallas kernels: 29.3 us -> 27.1 us  [run_fused(): pl.pallas_call(fused, out_shape=(jax.ShapeDtypeStruct((2 * BLK, D), BF16)...]
    unnamed x12 -> x10, local copies, waits for them, and re-layouts: 4.77 us -> 3.94 us
where the time goes in v3:
time: 175 us
  starting transfers between devices  54.9 us (31%)
  blocking collectives  51.9 us (30%)
  Pallas kernels  28.8 us (16%)
  waiting for transfers between devices  15.4 us (9%)
  between operations  15 us (9%)
  local copies, waits for them, and re-layouts  7.68 us (4%)
    pallas_call x1, Pallas kernels, run_fused(): pl.pallas_call(fused, out_shape=(jax.ShapeDtypeStruct((2 * BLK, D), BF16)...  27.1 us
    all_to_all x1, blocking collectives, reduce_all(): lax.all_to_all(jnp.broadcast_to(mine[None], (16,) + mine.shape), ('zh', '...  22.9 us
    ppermute x4, starting transfers between devices, gather_weight(): yb = [lax.ppermute(part, 'core', shift(2, 1)) for part in ya]  17.7 us
    all_to_all x1, blocking collectives, reduce_all(): lax.all_to_all(jnp.broadcast_to(mine[None], (32,) + mine.shape), plane, 0...  15.4 us
    all_to_all x1, blocking collectives, reduce_all(): parts = lax.all_to_all(packed.reshape(32, PACK // 32, 128), plane, 0, 0)  13.6 us
    ppermute x1, starting transfers between devices, gather_weight(): hn = lax.ppermute(heads, ('y', 'zl'), shift(32, -1))  12.1 us
    ppermute x1, starting transfers between devices, gather_weight(): far = lax.ppermute(quarter, ('zh', 'zl'), [(i, 15 - i) for i in range(16)])  12 us
    ppermute x1, waiting for transfers between devices, gather_weight(): far = lax.ppermute(quarter, ('zh', 'zl'), [(i, 15 - i) for i in range(16)])  7.9 us
  transfers between devices with their start and end apart: 12, of which 5 were waited for; matrix products, arithmetic and copies ran while one was open for 2% of the time, Pallas kernels for 1%

profile of v3, /device:TPU:1, one launch (start us, length us, event | category | flops | bytes accessed | tf_op | source)
XLA Modules:
  0.0 174.7 jit_solution(3418185898519532562)
XLA Ops:
  7.9 0.9 constant_dynamic-slice_fusion
  8.9 12.0 %collective-permute-start = (bf16[96,768]{1,0:T(8,128)(2,1)S(1)}, bf16[96,768]{1,0:T(8,128)(2,1)S(1)}, u32[]{:S(2)}, u32[]{:S(2)}) collective-permute-start(bf16[96,768]{1,0:T(8,128)(2,1)S(1)} %constant_dynamic-slice_fusion), channel_id=1, source_target_pairs={{0,263},{1,262},{2,261},{3,260},{4,259},{5,258},{6,257},{7,256},{2... | collective-permute-start | bytes 442376 | tf_op jit(solution)/shard_map/ppermute | solution.py:317
  22.2 1.1 copy-done
  23.4 1.1 copy-done.1
  25.3 1.0 pad_maximum_fusion.dw
  26.3 7.9 %collective-permute-done.src = bf16[96,768]{1,0:T(8,128)(2,1)S(1)} collective-permute-done((bf16[96,768]{1,0:T(8,128)(2,1)S(1)}, bf16[96,768]{1,0:T(8,128)(2,1)S(1)}, u32[]{:S(2)}, u32[]{:S(2)}) %collective-permute-start) | collective-permute-done | bytes 147488 | tf_op jit(solution)/shard_map/ppermute | solution.py:317
  35.0 4.0 %all-to-all-start = ((bf16[4,96,768]{2,1,0:T(8,128)(2,1)}), bf16[4,96,768]{2,1,0:T(8,128)(2,1)S(1)}, u32[]{:S(2)}, u32[]{:S(2)}) async-start(bf16[4,96,768]{2,1,0:T(8,128)(2,1)} %shard_map.119), calls=%async_computation | async-start | bytes 1179648 | tf_op jit(solution)/shard_map/all_to_all | solution.py:322
  39.1 1.9 %collective-permute-start.1 = (bf16[96,1536]{1,0:T(8,128)(2,1)S(1)}, bf16[96,1536]{1,0:T(8,128)(2,1)S(1)}, u32[]{:S(2)}, u32[]{:S(2)}) collective-permute-start(bf16[96,1536]{1,0:T(8,128)(2,1)S(1)} %get-tuple-element.20), channel_id=1, source_target_pairs={{0,1},{1,2},{2,3},{3,4},{4,5},{5,6},{6,7},{7,8},{8,9},{9,10},{10,1... | collective-permute-start | bytes 884744 | tf_op jit(solution)/shard_map/ppermute | solution.py:320
  41.0 12.1 %collective-permute-start.2 = (bf16[96,1536]{1,0:T(8,128)(2,1)S(1)}, bf16[96,1536]{1,0:T(8,128)(2,1)S(1)}, u32[]{:S(2)}, u32[]{:S(2)}) collective-permute-start(bf16[96,1536]{1,0:T(8,128)(2,1)S(1)} %get-tuple-element.21), channel_id=1, source_target_pairs={{0,31},{1,0},{2,1},{3,2},{4,3},{5,4},{6,5},{7,6},{8,7},{9,8},{10,9... | collective-permute-start | bytes 884744 | tf_op jit(solution)/shard_map/ppermute | solution.py:321
  53.1 4.0 %collective-permute-done.1.hp = bf16[96,1536]{1,0:T(8,128)(2,1)S(1)} collective-permute-done((bf16[96,1536]{1,0:T(8,128)(2,1)S(1)}, bf16[96,1536]{1,0:T(8,128)(2,1)S(1)}, u32[]{:S(2)}, u32[]{:S(2)}) %collective-permute-start.1) | collective-permute-done | bytes 294944 | tf_op jit(solution)/shard_map/ppermute | solution.py:320
  58.6 3.4 %collective-permute-start.5 = (bf16[384,768]{1,0:T(8,128)(2,1)S(1)}, bf16[384,768]{1,0:T(8,128)(2,1)S(1)}, u32[]{:S(2)}, u32[]{:S(2)}) collective-permute-start(bf16[384,768]{1,0:T(8,128)(2,1)S(1)} %bitcast.27), channel_id=1, source_target_pairs={{0,24},{8,0},{16,8},{24,16},{1,25},{9,1},{17,9},{25,17},{2,26},{10... | collective-permute-start | bytes 1769480 | tf_op jit(solution)/shard_map/ppermute | solution.py:329
  62.0 1.9 %collective-permute-start.4 = (bf16[384,768]{1,0:T(8,128)(2,1)S(1)}, bf16[384,768]{1,0:T(8,128)(2,1)S(1)}, u32[]{:S(2)}, u32[]{:S(2)}) collective-permute-start(bf16[384,768]{1,0:T(8,128)(2,1)S(1)} %bitcast.28), channel_id=1, source_target_pairs={{0,1},{1,0},{2,3},{3,2},{4,5},{5,4},{6,7},{7,6},{8,9},{9,8},{10,11... | collective-permute-start | bytes 1769480 | tf_op jit(solution)/shard_map/ppermute | solution.py:328
  63.9 1.9 %collective-permute-start.3 = (bf16[384,768]{1,0:T(8,128)(2,1)S(1)}, bf16[384,768]{1,0:T(8,128)(2,1)S(1)}, u32[]{:S(2)}, u32[]{:S(2)}) collective-permute-start(bf16[384,768]{1,0:T(8,128)(2,1)S(1)} %bitcast.29), channel_id=1, source_target_pairs={{0,8},{8,16},{16,24},{24,0},{1,9},{9,17},{17,25},{25,1},{2,10},{10... | collective-permute-start | bytes 1769480 | tf_op jit(solution)/shard_map/ppermute | solution.py:327
  65.9 5.3 %collective-permute-start.6 = (bf16[384,768]{1,0:T(8,128)(2,1)S(1)}, bf16[384,768]{1,0:T(8,128)(2,1)S(1)}, u32[]{:S(2)}, u32[]{:S(2)}) collective-permute-start(bf16[384,768]{1,0:T(8,128)(2,1)S(1)} %bitcast.30), channel_id=1, source_target_pairs={{0,32},{32,0},{1,33},{33,1},{2,34},{34,2},{3,35},{35,3},{4,36},{36... | collective-permute-start | bytes 1769480 | tf_op jit(solution)/shard_map/ppermute | solution.py:331
  71.2 1.1 collective-permute-done.5.ya3
  72.3 5.8 %collective-permute-start.9 = (bf16[384,768]{1,0:T(8,128)(2,1)S(1)}, bf16[384,768]{1,0:T(8,128)(2,1)}, u32[]{:S(2)}, u32[]{:S(2)}) collective-permute-start(bf16[384,768]{1,0:T(8,128)(2,1)S(1)} %collective-permute-done.5.ya3), channel_id=1, source_target_pairs={{0,32},{32,0},{1,33},{33,1},{2,34},{34,2},{3,35},{35,3},{4,36},{36... | collective-permute-start | bytes 1769480 | tf_op jit(solution)/shard_map/ppermute | solution.py:331
  78.1 3.4 %collective-permute-start.8 = (bf16[384,768]{1,0:T(8,128)(2,1)S(1)}, bf16[384,768]{1,0:T(8,128)(2,1)}, u32[]{:S(2)}, u32[]{:S(2)}) collective-permute-start(bf16[384,768]{1,0:T(8,128)(2,1)S(1)} %collective-permute-done.4.ya2), channel_id=1, source_target_pairs={{0,32},{32,0},{1,33},{33,1},{2,34},{34,2},{3,35},{35,3},{4,36},{36... | collective-permute-start | bytes 1769480 | tf_op jit(solution)/shard_map/ppermute | solution.py:331
  81.6 3.1 %collective-permute-start.7 = (bf16[384,768]{1,0:T(8,128)(2,1)S(1)}, bf16[384,768]{1,0:T(8,128)(2,1)}, u32[]{:S(2)}, u32[]{:S(2)}) collective-permute-start(bf16[384,768]{1,0:T(8,128)(2,1)S(1)} %collective-permute-done.3.ya1), channel_id=1, source_target_pairs={{0,32},{32,0},{1,33},{33,1},{2,34},{34,2},{3,35},{35,3},{4,36},{36... | collective-permute-start | bytes 1769480 | tf_op jit(solution)/shard_map/ppermute | solution.py:331
  85.5 0.9 collective-permute-done.7.yb1
  86.4 1.0 copy-done.3
  87.4 27.1 %shard_map.121 = (bf16[256,1536]{1,0:T(8,128)(2,1)}, bf16[256,1536]{1,0:T(8,128)(2,1)}, f32[512,128]{1,0:T(8,128)S(1)}) custom-call(s32[8]{0:T(128)S(1)} %stack.22.sc, bf16[256,1536]{1,0:T(8,128)(2,1)} %bitcast.23, bf16[256,1536]{1,0:T(8,128)(2,1)} %bitcast.25, bf16[96,1536]{1,0:T(8,128)(2,1)S(1)} %collective-permute-done.1.hp, ...), custom_call_target="tpu_custom_call" | custom-call | flops 8999999488 | bytes 14000000 | tf_op jit(solution)/shard_map/pallas_call | solution.py:235
  114.5 13.6 %all_to_all.20 = f32[32,16,128]{2,1,0:T(8,128)S(1)} all-to-all(f32[32,16,128]{2,1,0:T(8,128)S(1)} %bitcast.32), channel_id=1, replica_groups=mesh['zh'=2,'x'=4,'core'=2,'y'=4,'zl'=8] {'x','core','y'}, dimensions={0} | all-to-all | bytes 524288 | tf_op jit(solution)/shard_map/all_to_all | solution.py:337
  128.2 22.9 %all_to_all.21 = f32[16,16,128]{2,1,0:T(8,128)S(1)} all-to-all(f32[16,16,128]{2,1,0:T(8,128)S(1)} %broadcast_in_dim.20), channel_id=1, replica_groups=mesh['zh'=2,'x'=4,'core'=2,'y'=4,'zl'=8] {'zh','zl'}, dimensions={0} | all-to-all | bytes 262144 | tf_op jit(solution)/shard_map/all_to_all | solution.py:339
  151.2 15.4 %all_to_all.22 = f32[32,16,128]{2,1,0:T(8,128)S(1)} all-to-all(f32[32,16,128]{2,1,0:T(8,128)S(1)} %broadcast_in_dim.21), channel_id=1, replica_groups=mesh['zh'=2,'x'=4,'core'=2,'y'=4,'zl'=8] {'x','core','y'}, dimensions={0} | all-to-all | bytes 524288 | tf_op jit(solution)/shard_map/all_to_all | solution.py:341
  (28 shorter events, 6.8 us)
Async XLA Ops:
  7.2 77.5 %copy-start.4 = (s32[1,64]{1,0:T(1,128)S(1)}, s32[1,64]{1,0:T(1,128)}, u32[]{:S(2)}) copy-start(s32[1,64]{1,0:T(1,128)} %param.10) | copy-start | bytes 772
  7.2 79.3 %all-gather.2.cloned.1.call-start = ((), (), s32[]{:S(2)}) async-start(), calls=%async_computation.4 | async-start | bytes 5308416 | tf_op jit(solution)/shard_map/all_gather | solution.py:316
  8.9 25.3 %collective-permute-start = (bf16[96,768]{1,0:T(8,128)(2,1)S(1)}, bf16[96,768]{1,0:T(8,128)(2,1)S(1)}, u32[]{:S(2)}, u32[]{:S(2)}) collective-permute-start(bf16[96,768]{1,0:T(8,128)(2,1)S(1)} %constant_dynamic-slice_fusion), channel_id=1, source_target_pairs={{0,263},{1,262},{2,261},{3,260},{4,259},{5,258},{6,257},{7,256},{2... | collective-permute-start | bytes 442376 | tf_op jit(solution)/shard_map/ppermute | solution.py:317
  22.2 1.1 copy-start
  23.4 1.1 copy-start.1
  35.0 23.5 %all-to-all-start = ((bf16[4,96,768]{2,1,0:T(8,128)(2,1)}), bf16[4,96,768]{2,1,0:T(8,128)(2,1)S(1)}, u32[]{:S(2)}, u32[]{:S(2)}) async-start(bf16[4,96,768]{2,1,0:T(8,128)(2,1)} %shard_map.119), calls=%async_computation | async-start | bytes 1179648 | tf_op jit(solution)/shard_map/all_to_all | solution.py:322
  39.1 18.0 %collective-permute-start.1 = (bf16[96,1536]{1,0:T(8,128)(2,1)S(1)}, bf16[96,1536]{1,0:T(8,128)(2,1)S(1)}, u32[]{:S(2)}, u32[]{:S(2)}) collective-permute-start(bf16[96,1536]{1,0:T(8,128)(2,1)S(1)} %get-tuple-element.20), channel_id=1, source_target_pairs={{0,1},{1,2},{2,3},{3,4},{4,5},{5,6},{6,7},{7,8},{8,9},{9,10},{10,1... | collective-permute-start | bytes 884744 | tf_op jit(solution)/shard_map/ppermute | solution.py:320
  41.0 16.9 %collective-permute-start.2 = (bf16[96,1536]{1,0:T(8,128)(2,1)S(1)}, bf16[96,1536]{1,0:T(8,128)(2,1)S(1)}, u32[]{:S(2)}, u32[]{:S(2)}) collective-permute-start(bf16[96,1536]{1,0:T(8,128)(2,1)S(1)} %get-tuple-element.21), channel_id=1, source_target_pairs={{0,31},{1,0},{2,1},{3,2},{4,3},{5,4},{6,5},{7,6},{8,7},{9,8},{10,9... | collective-permute-start | bytes 884744 | tf_op jit(solution)/shard_map/ppermute | solution.py:321
  57.9 0.7 copy-start.2
  58.6 13.8 %collective-permute-start.5 = (bf16[384,768]{1,0:T(8,128)(2,1)S(1)}, bf16[384,768]{1,0:T(8,128)(2,1)S(1)}, u32[]{:S(2)}, u32[]{:S(2)}) collective-permute-start(bf16[384,768]{1,0:T(8,128)(2,1)S(1)} %bitcast.27), channel_id=1, source_target_pairs={{0,24},{8,0},{16,8},{24,16},{1,25},{9,1},{17,9},{25,17},{2,26},{10... | collective-permute-start | bytes 1769480 | tf_op jit(solution)/shard_map/ppermute | solution.py:329
  62.0 16.1 %collective-permute-start.4 = (bf16[384,768]{1,0:T(8,128)(2,1)S(1)}, bf16[384,768]{1,0:T(8,128)(2,1)S(1)}, u32[]{:S(2)}, u32[]{:S(2)}) collective-permute-start(bf16[384,768]{1,0:T(8,128)(2,1)S(1)} %bitcast.28), channel_id=1, source_target_pairs={{0,1},{1,0},{2,3},{3,2},{4,5},{5,4},{6,7},{7,6},{8,9},{9,8},{10,11... | collective-permute-start | bytes 1769480 | tf_op jit(solution)/shard_map/ppermute | solution.py:328
  63.9 17.6 %collective-permute-start.3 = (bf16[384,768]{1,0:T(8,128)(2,1)S(1)}, bf16[384,768]{1,0:T(8,128)(2,1)S(1)}, u32[]{:S(2)}, u32[]{:S(2)}) collective-permute-start(bf16[384,768]{1,0:T(8,128)(2,1)S(1)} %bitcast.29), channel_id=1, source_target_pairs={{0,8},{8,16},{16,24},{24,0},{1,9},{9,17},{17,25},{25,1},{2,10},{10... | collective-permute-start | bytes 1769480 | tf_op jit(solution)/shard_map/ppermute | solution.py:327
  65.9 19.6 %collective-permute-start.6 = (bf16[384,768]{1,0:T(8,128)(2,1)S(1)}, bf16[384,768]{1,0:T(8,128)(2,1)S(1)}, u32[]{:S(2)}, u32[]{:S(2)}) collective-permute-start(bf16[384,768]{1,0:T(8,128)(2,1)S(1)} %bitcast.30), channel_id=1, source_target_pairs={{0,32},{32,0},{1,33},{33,1},{2,34},{34,2},{3,35},{35,3},{4,36},{36... | collective-permute-start | bytes 1769480 | tf_op jit(solution)/shard_map/ppermute | solution.py:331
  72.3 13.2 %collective-permute-start.9 = (bf16[384,768]{1,0:T(8,128)(2,1)S(1)}, bf16[384,768]{1,0:T(8,128)(2,1)}, u32[]{:S(2)}, u32[]{:S(2)}) collective-permute-start(bf16[384,768]{1,0:T(8,128)(2,1)S(1)} %collective-permute-done.5.ya3), channel_id=1, source_target_pairs={{0,32},{32,0},{1,33},{33,1},{2,34},{34,2},{3,35},{35,3},{4,36},{36... | collective-permute-start | bytes 1769480 | tf_op jit(solution)/shard_map/ppermute | solution.py:331
  78.1 7.4 %collective-permute-start.8 = (bf16[384,768]{1,0:T(8,128)(2,1)S(1)}, bf16[384,768]{1,0:T(8,128)(2,1)}, u32[]{:S(2)}, u32[]{:S(2)}) collective-permute-start(bf16[384,768]{1,0:T(8,128)(2,1)S(1)} %collective-permute-done.4.ya2), channel_id=1, source_target_pairs={{0,32},{32,0},{1,33},{33,1},{2,34},{34,2},{3,35},{35,3},{4,36},{36... | collective-permute-start | bytes 1769480 | tf_op jit(solution)/shard_map/ppermute | solution.py:331
  81.6 4.9 %collective-permute-start.7 = (bf16[384,768]{1,0:T(8,128)(2,1)S(1)}, bf16[384,768]{1,0:T(8,128)(2,1)}, u32[]{:S(2)}, u32[]{:S(2)}) collective-permute-start(bf16[384,768]{1,0:T(8,128)(2,1)S(1)} %collective-permute-done.3.ya1), channel_id=1, source_target_pairs={{0,32},{32,0},{1,33},{33,1},{2,34},{34,2},{3,35},{35,3},{4,36},{36... | collective-permute-start | bytes 1769480 | tf_op jit(solution)/shard_map/ppermute | solution.py:331
  86.4 1.0 copy-start.3
Sparse Core Ops, SparseCore 0:
  10.1 53.9 all-gather.1

commit v4 on v3

--- a/solution.py
+++ b/solution.py
@@ -12,6 +12,7 @@
 EXT = BLK + 2 * HX
 HG = 16
 EXG = BLK + 2 * HG
+RIM = HX + HG
 SHARD = 96
 HALF = 768
 QUART = 768
@@ -32,7 +33,7 @@
     return [(i, (i + by) % count) for i in range(count)]
 
 
-def fused(sc, x_hbm, og_hbm, hp, hn, dw, near, ya0, ya1, ya2, ya3, yb0, yb1, yb2, yb3,
+def fused(sc, x_hbm, og_hbm, rim_a, rim_b, dw, near, ya0, ya1, ya2, ya3, yb0, yb1, yb2, yb3,
           act_ref, ig_ref, red_ref,
           xe, oge, w, nrm, std, inv, gbuf, abuf, sbuf, slp, kacc, gh, gn,
           xsem, wsem):
@@ -46,16 +47,31 @@
         c.start()
         bag.append(c)
 
+    even = sc[5] == 0
+
+    def pick(when_even, when_odd, rows, dst, sem):
+        @pl.when(even)
+        def _():
+            pltpu.make_async_copy(when_even.at[rows], dst, sem).start()
+
+        @pl.when(jnp.logical_not(even))
+        def _():
+            pltpu.make_async_copy(when_odd.at[rows], dst, sem).start()
+
+        xcopies.append(pltpu.make_async_copy(when_odd.at[rows], dst, sem))
+
     for s in range(2):
         before = jnp.maximum(s - jnp.where(pos == 0, 1, 0), 0)
         after = jnp.minimum(s + jnp.where(pos == 31, 1, 0), 1)
+        hp = pl.multiple_of(before * RIM, 16)
+        hn = pl.multiple_of(after * RIM, 16)
         n = 6 * s
         go(x_hbm.at[pl.ds(s * BLK, BLK)], xe.at[pl.ds(s * EXT + HX, BLK)], xsem.at[n], xcopies)
-        go(hp.at[pl.ds(pl.multiple_of(before * HX, HX), HX)], xe.at[pl.ds(s * EXT, HX)], xsem.at[n + 1], xcopies)
-        go(hn.at[pl.ds(pl.multiple_of(after * HX, HX), HX)], xe.at[pl.ds(s * EXT + HX + BLK, HX)], xsem.at[n + 2], xcopies)
+        pick(rim_b, rim_a, pl.ds(hp, HX), xe.at[pl.ds(s * EXT, HX)], xsem.at[n + 1])
+        pick(rim_a, rim_b, pl.ds(hn, HX), xe.at[pl.ds(s * EXT + HX + BLK, HX)], xsem.at[n + 2])
         go(og_hbm.at[pl.ds(s * BLK, BLK)], oge.at[pl.ds(s * EXG + HG, BLK)], xsem.at[n + 3], xcopies)
-        go(hp.at[pl.ds(pl.multiple_of(2 * HX + before * HG, HG), HG)], oge.at[pl.ds(s * EXG, HG)], xsem.at[n + 4], xcopies)
-        go(hn.at[pl.ds(pl.multiple_of(2 * HX + after * HG, HG), HG)], oge.at[pl.ds(s * EXG + HG + BLK, HG)], xsem.at[n + 5], xcopies)
+        pick(rim_b, rim_a, pl.ds(hp + HX, HG), oge.at[pl.ds(s * EXG, HG)], xsem.at[n + 4])
+        pick(rim_a, rim_b, pl.ds(hn + HX, HG), oge.at[pl.ds(s * EXG + HG + BLK, HG)], xsem.at[n + 5])
 
     wcopies = []
 
@@ -229,7 +245,7 @@
         red_ref[BIAS_ROW + l:BIAS_ROW + l + 1, :] = brow[:, l * 128:(l + 1) * 128]
 
 
-def run_fused(scalars, frames, out_grad, hp, hn, params, pieces):
+def run_fused(scalars, frames, out_grad, rim_a, rim_b, params, pieces):
     any_spec = pl.BlockSpec(memory_space=pltpu.HBM)
     vm = pl.BlockSpec(memory_space=pltpu.VMEM)
     return pl.pallas_call(
@@ -258,35 +274,42 @@
             pltpu.SemaphoreType.DMA((12,)),
             pltpu.SemaphoreType.DMA((40,)),
         ],
-        compiler_params=pltpu.CompilerParams(vmem_limit_bytes=48 * 1024 * 1024),
+        compiler_params=pltpu.CompilerParams(vmem_limit_bytes=51 * 1024 * 1024),
         cost_estimate=pl.CostEstimate(flops=9_000_000_000, bytes_accessed=14_000_000, transcendentals=2_000_000),
-    )(scalars, frames, out_grad, hp, hn, params, *pieces)
-
-
-def take_rims(x, g, tails, heads, sem):
+    )(scalars, frames, out_grad, rim_a, rim_b, params, *pieces)
+
+
+def take_rims(sc, x, g, near, far, sem):
+    even = sc[5] == 0
     copies = []
-    for dst, fx, fg in ((tails, BLK - HX, BLK - HG), (heads, 0, 0)):
-        for s in range(2):
-            copies.append(pltpu.make_async_copy(x.at[pl.ds(s * BLK + fx, HX)], dst.at[pl.ds(s * HX, HX)], sem.at[len(copies)]))
-            copies.append(pltpu.make_async_copy(g.at[pl.ds(s * BLK + fg, HG)], dst.at[pl.ds(2 * HX + s * HG, HG)], sem.at[len(copies)]))
-    for c in copies:
-        c.start()
+
+    def go(src, dst):
+        copies.append(pltpu.make_async_copy(src, dst, sem.at[len(copies)]))
+        copies[-1].start()
+
+    for s in range(2):
+        last = s * BLK + BLK
+        for dst, tail in ((near, even), (far, jnp.logical_not(even))):
+            fx = pl.multiple_of(jnp.where(tail, last - HX, s * BLK), 16)
+            fg = pl.multiple_of(jnp.where(tail, last - HG, s * BLK), 16)
+            go(x.at[pl.ds(fx, HX)], dst.at[pl.ds(s * RIM, HX)])
+            go(g.at[pl.ds(fg, HG)], dst.at[pl.ds(s * RIM + HX, HG)])
     for c in copies:
         c.wait()
 
 
-def rims(x, g):
-    any_spec = pl.BlockSpec(memory_space=pltpu.HBM)
-    shape = jax.ShapeDtypeStruct((2 * (HX + HG), D), BF16)
+def rims(scalars, x, g):
+    any_spec = pl.BlockSpec(memory_space=pl.ANY)
+    both = jax.ShapeDtypeStruct((2 * RIM, D), BF16)
     return pl.pallas_call(
         take_rims,
-        out_shape=(shape, shape),
-        in_specs=[any_spec] * 2,
+        out_shape=(both, both),
+        in_specs=[pl.BlockSpec(memory_space=pltpu.SMEM), any_spec, any_spec],
         out_specs=(any_spec, any_spec),
         scratch_shapes=[pltpu.SemaphoreType.DMA((8,))],
         compiler_params=pltpu.CompilerParams(vmem_limit_bytes=1024 * 1024),
-        cost_estimate=pl.CostEstimate(flops=0, bytes_accessed=30_000_000, transcendentals=0),
-    )(x, g)
+        cost_estimate=pl.CostEstimate(flops=0, bytes_accessed=1_200_000, transcendentals=0),
+    )(scalars, x, g)
 
 
 def write_copies(src, dst, sem):
@@ -310,17 +333,24 @@
     )(part)
 
 
-def gather_weight(own, turn, tails, heads, params):
+def meet_next():
+    pairs = []
+    for i in range(1, 32, 2):
+        pairs += [(i, (i + 1) % 32), ((i + 1) % 32, i)]
+    return pairs
+
+
+def gather_weight(own, turn, rim_a, rim_b, params):
     theirs = lax.rem(turn + 2, 4)
     quarter = lax.dynamic_slice_in_dim(own, theirs * QUART, QUART, axis=1)
     near = lax.all_gather(own, ("x", "core"), axis=0, tiled=True)
     far = lax.ppermute(quarter, ("zh", "zl"), [(i, 15 - i) for i in range(16)])
     far = four_copies(far)
-    far, tails, heads, params = lax.optimization_barrier((far, tails, heads, params))
-    hp = lax.ppermute(tails, ("y", "zl"), shift(32, 1))
-    hn = lax.ppermute(heads, ("y", "zl"), shift(32, -1))
+    far, rim_a, rim_b, params = lax.optimization_barrier((far, rim_a, rim_b, params))
+    a = lax.ppermute(rim_a, ("y", "zl"), [(i, i ^ 1) for i in range(32)])
+    b = lax.ppermute(rim_b, ("y", "zl"), meet_next())
     far = lax.all_to_all(far, "x", 0, 0)
-    far, hp, hn = lax.optimization_barrier((far, hp, hn))
+    far, a, b = lax.optimization_barrier((far, a, b))
     far = far.reshape(4 * SHARD, QUART)
     ya = [
         far,
@@ -329,7 +359,7 @@
         lax.ppermute(far, "y", shift(4, -1)),
     ]
     yb = [lax.ppermute(part, "core", shift(2, 1)) for part in ya]
-    return hp, hn, params, [near] + ya + yb
+    return a, b, params, [near] + ya + yb
 
 
 def reduce_all(packed):
@@ -351,13 +381,13 @@
     seq = idx("y") * 8 + idx("zl")
     position = jnp.mod(seq - owner_map[0, 0], 32)
     turn = lax.rem(idx("y") + 2 * lax.rem(idx("zl"), 2), 4)
-    scalars = jnp.stack([position, lengths[0], idx("zh"), idx("core"), turn, position, position, position]).astype(jnp.int32)
-
-    tails, heads = rims(x, dy)
+    scalars = jnp.stack([position, lengths[0], idx("zh"), idx("core"), turn, lax.rem(idx("zl"), 2), position, position]).astype(jnp.int32)
+
+    rim_a, rim_b = rims(scalars, x, dy)
     params = jnp.concatenate([dw_kernel, norm_gain[None], norm_bias[None]], axis=0)
-    hp, hn, params, pieces = gather_weight(proj_weight, turn, tails, heads, params)
+    rim_a, rim_b, params, pieces = gather_weight(proj_weight, turn, rim_a, rim_b, params)
     act, ig, packed = run_fused(
-        scalars, x, dy, hp, hn, params, pieces)
+        scalars, x, dy, rim_a, rim_b, params, pieces)
     kernel_grad, gain_grad, bias_grad = reduce_all(packed)
     return act.reshape(1, 2 * BLK, D), ig.reshape(1, 2 * BLK, D), kernel_grad, gain_grad, bias_grad
 

time: 175 us -> 171 us (0.977)
  starting transfers between devices: 54.9 us -> 47.8 us
  waiting for transfers between devices: 15.4 us -> 21.1 us
  blocking collectives: 51.9 us -> 47.4 us
    ppermute x2, waiting for transfers between devices: 4.8 us -> 10.8 us  [the longest x1 10.8 us: gather_weight(): b = lax.ppermute(rim_b, ('y', 'zl'), meet_next())]
    all_to_all x1, blocking collectives: 22.9 us -> 18.4 us  [reduce_all(): lax.all_to_all(jnp.broadcast_to(mine[None], (16,) + mine.shape), ('zh', '...]
    ppermute x4, starting transfers between devices: 17.7 us -> 13.8 us  [gather_weight(): yb = [lax.ppermute(part, 'core', shift(2, 1)) for part in ya]]
    ppermute x2, starting transfers between devices: 14 us -> 10.8 us  [the longest x1 8.94 us: gather_weight(): b = lax.ppermute(rim_b, ('y', 'zl'), meet_next())]
    ppermute x1, waiting for transfers between devices: 1.11 us -> 3.72 us  [gather_weight(): lax.ppermute(far, 'y', shift(4, -1))]
    ppermute x1, waiting for transfers between devices: 7.9 us -> 5.9 us  [gather_weight(): far = lax.ppermute(quarter, ('zh', 'zl'), [(i, 15 - i) for i in range(16)])]
    unnamed x10 -> x12, local copies, waits for them, and re-layouts: 3.94 us -> 4.09 us
  transfers between devices with their start and end apart: 12 -> 12, of which waited for: 5 -> 3; matrix products, arithmetic and copies ran while one was open for 2% -> 2% of each run, Pallas kernels for 1% -> 1%
where the time goes in v4:
time: 171 us; the launch traced here: 170 us
  starting transfers between devices  47.8 us (28%)
  blocking collectives  47.4 us (28%)
  Pallas kernels  29.7 us (17%)
  waiting for transfers between devices  21.1 us (12%)
  between operations  15.6 us (9%)
  local copies, waits for them, and re-layouts  7.83 us (5%)
    pallas_call x1, Pallas kernels, run_fused(): pl.pallas_call(fused, out_shape=(jax.ShapeDtypeStruct((2 * BLK, D), BF16)...  27.5 us
    all_to_all x1, blocking collectives, reduce_all(): lax.all_to_all(jnp.broadcast_to(mine[None], (16,) + mine.shape), ('zh', '...  18.4 us
    all_to_all x1, blocking collectives, reduce_all(): lax.all_to_all(jnp.broadcast_to(mine[None], (32,) + mine.shape), plane, 0...  15.4 us
    ppermute x4, starting transfers between devices, gather_weight(): yb = [lax.ppermute(part, 'core', shift(2, 1)) for part in ya]  13.8 us
    all_to_all x1, blocking collectives, reduce_all(): parts = lax.all_to_all(packed.reshape(32, PACK // 32, 128), plane, 0, 0)  13.6 us
    ppermute x1, starting transfers between devices, gather_weight(): far = lax.ppermute(quarter, ('zh', 'zl'), [(i, 15 - i) for i in range(16)])  12 us
    ppermute x1, waiting for transfers between devices, gather_weight(): b = lax.ppermute(rim_b, ('y', 'zl'), meet_next())  10.8 us
    ppermute x1, starting transfers between devices, gather_weight(): b = lax.ppermute(rim_b, ('y', 'zl'), meet_next())  8.94 us
  transfers between devices with their start and end apart: 12, of which 3 were waited for; matrix products, arithmetic and copies ran while one was open for 2% of the time, Pallas kernels for 1%

profile of v4, /device:TPU:1, one launch (start us, length us, event | category | flops | bytes accessed | tf_op | source)
XLA Modules:
  0.0 170.5 jit_solution(7200033674228314680)
XLA Ops:
  7.9 0.9 constant_dynamic-slice_fusion
  8.9 12.0 %collective-permute-start = (bf16[96,768]{1,0:T(8,128)(2,1)S(1)}, bf16[96,768]{1,0:T(8,128)(2,1)S(1)}, u32[]{:S(2)}, u32[]{:S(2)}) collective-permute-start(bf16[96,768]{1,0:T(8,128)(2,1)S(1)} %constant_dynamic-slice_fusion), channel_id=1, source_target_pairs={{0,263},{1,262},{2,261},{3,260},{4,259},{5,258},{6,257},{7,256},{2... | collective-permute-start | bytes 442376 | tf_op jit(solution)/shard_map/ppermute | solution.py:347
  23.6 1.1 copy-done
  24.8 1.1 copy-done.1
  25.9 1.4 shard_map.120
  27.3 1.0 pad_maximum_fusion.dw
  28.3 5.9 %collective-permute-done.src = bf16[96,768]{1,0:T(8,128)(2,1)S(1)} collective-permute-done((bf16[96,768]{1,0:T(8,128)(2,1)S(1)}, bf16[96,768]{1,0:T(8,128)(2,1)S(1)}, u32[]{:S(2)}, u32[]{:S(2)}) %collective-permute-start) | collective-permute-done | bytes 147488 | tf_op jit(solution)/shard_map/ppermute | solution.py:347
  34.2 0.8 shard_map.119
  35.0 4.0 %all-to-all-start = ((bf16[4,96,768]{2,1,0:T(8,128)(2,1)}), bf16[4,96,768]{2,1,0:T(8,128)(2,1)S(1)}, u32[]{:S(2)}, u32[]{:S(2)}) async-start(bf16[4,96,768]{2,1,0:T(8,128)(2,1)} %shard_map.119), calls=%async_computation | async-start | bytes 1179648 | tf_op jit(solution)/shard_map/all_to_all | solution.py:352
  39.0 1.9 %collective-permute-start.1 = (bf16[96,1536]{1,0:T(8,128)(2,1)S(1)}, bf16[96,1536]{1,0:T(8,128)(2,1)S(1)}, u32[]{:S(2)}, u32[]{:S(2)}) collective-permute-start(bf16[96,1536]{1,0:T(8,128)(2,1)S(1)} %get-tuple-element.20), channel_id=1, source_target_pairs={{0,1},{1,0},{2,3},{3,2},{4,5},{5,4},{6,7},{7,6},{8,9},{9,8},{10,11... | collective-permute-start | bytes 884744 | tf_op jit(solution)/shard_map/ppermute | solution.py:350
  41.0 8.9 %collective-permute-start.2 = (bf16[96,1536]{1,0:T(8,128)(2,1)S(1)}, bf16[96,1536]{1,0:T(8,128)(2,1)S(1)}, u32[]{:S(2)}, u32[]{:S(2)}) collective-permute-start(bf16[96,1536]{1,0:T(8,128)(2,1)S(1)} %get-tuple-element.21), channel_id=1, source_target_pairs={{1,2},{2,1},{3,4},{4,3},{5,6},{6,5},{7,8},{8,7},{9,10},{10,9},{11,... | collective-permute-start | bytes 884744 | tf_op jit(solution)/shard_map/ppermute | solution.py:351
  49.9 10.8 %collective-permute-done.2.rim_b = bf16[96,1536]{1,0:T(8,128)(2,1)S(1)} collective-permute-done((bf16[96,1536]{1,0:T(8,128)(2,1)S(1)}, bf16[96,1536]{1,0:T(8,128)(2,1)S(1)}, u32[]{:S(2)}, u32[]{:S(2)}) %collective-permute-start.2) | collective-permute-done | bytes 294944 | tf_op jit(solution)/shard_map/ppermute | solution.py:351
  60.7 2.1 %collective-permute-start.5 = (bf16[384,768]{1,0:T(8,128)(2,1)S(1)}, bf16[384,768]{1,0:T(8,128)(2,1)S(1)}, u32[]{:S(2)}, u32[]{:S(2)}) collective-permute-start(bf16[384,768]{1,0:T(8,128)(2,1)S(1)} %bitcast.28), channel_id=1, source_target_pairs={{0,24},{8,0},{16,8},{24,16},{1,25},{9,1},{17,9},{25,17},{2,26},{10... | collective-permute-start | bytes 1769480 | tf_op jit(solution)/shard_map/ppermute | solution.py:359
  62.8 1.9 %collective-permute-start.4 = (bf16[384,768]{1,0:T(8,128)(2,1)S(1)}, bf16[384,768]{1,0:T(8,128)(2,1)S(1)}, u32[]{:S(2)}, u32[]{:S(2)}) collective-permute-start(bf16[384,768]{1,0:T(8,128)(2,1)S(1)} %bitcast.29), channel_id=1, source_target_pairs={{0,1},{1,0},{2,3},{3,2},{4,5},{5,4},{6,7},{7,6},{8,9},{9,8},{10,11... | collective-permute-start | bytes 1769480 | tf_op jit(solution)/shard_map/ppermute | solution.py:358
  64.7 3.2 %collective-permute-start.3 = (bf16[384,768]{1,0:T(8,128)(2,1)S(1)}, bf16[384,768]{1,0:T(8,128)(2,1)S(1)}, u32[]{:S(2)}, u32[]{:S(2)}) collective-permute-start(bf16[384,768]{1,0:T(8,128)(2,1)S(1)} %bitcast.30), channel_id=1, source_target_pairs={{0,8},{8,16},{16,24},{24,0},{1,9},{9,17},{17,25},{25,1},{2,10},{10... | collective-permute-start | bytes 1769480 | tf_op jit(solution)/shard_map/ppermute | solution.py:357
  67.9 4.1 %collective-permute-start.6 = (bf16[384,768]{1,0:T(8,128)(2,1)S(1)}, bf16[384,768]{1,0:T(8,128)(2,1)S(1)}, u32[]{:S(2)}, u32[]{:S(2)}) collective-permute-start(bf16[384,768]{1,0:T(8,128)(2,1)S(1)} %bitcast.31), channel_id=1, source_target_pairs={{0,32},{32,0},{1,33},{33,1},{2,34},{34,2},{3,35},{35,3},{4,36},{36... | collective-permute-start | bytes 1769480 | tf_op jit(solution)/shard_map/ppermute | solution.py:361
  72.0 3.7 %collective-permute-done.5.ya3 = bf16[384,768]{1,0:T(8,128)(2,1)S(1)} collective-permute-done((bf16[384,768]{1,0:T(8,128)(2,1)S(1)}, bf16[384,768]{1,0:T(8,128)(2,1)S(1)}, u32[]{:S(2)}, u32[]{:S(2)}) %collective-permute-start.5) | collective-permute-done | bytes 589856 | tf_op jit(solution)/shard_map/ppermute | solution.py:359
  75.8 4.5 %collective-permute-start.9 = (bf16[384,768]{1,0:T(8,128)(2,1)S(1)}, bf16[384,768]{1,0:T(8,128)(2,1)S(1)}, u32[]{:S(2)}, u32[]{:S(2)}) collective-permute-start(bf16[384,768]{1,0:T(8,128)(2,1)S(1)} %collective-permute-done.5.ya3), channel_id=1, source_target_pairs={{0,32},{32,0},{1,33},{33,1},{2,34},{34,2},{3,35},{35,3},{4,36},{36... | collective-permute-start | bytes 1769480 | tf_op jit(solution)/shard_map/ppermute | solution.py:361
  80.3 2.1 %collective-permute-start.8 = (bf16[384,768]{1,0:T(8,128)(2,1)S(1)}, bf16[384,768]{1,0:T(8,128)(2,1)S(1)}, u32[]{:S(2)}, u32[]{:S(2)}) collective-permute-start(bf16[384,768]{1,0:T(8,128)(2,1)S(1)} %collective-permute-done.4.ya2), channel_id=1, source_target_pairs={{0,32},{32,0},{1,33},{33,1},{2,34},{34,2},{3,35},{35,3},{4,36},{36... | collective-permute-start | bytes 1769480 | tf_op jit(solution)/shard_map/ppermute | solution.py:361
  82.3 3.1 %collective-permute-start.7 = (bf16[384,768]{1,0:T(8,128)(2,1)S(1)}, bf16[384,768]{1,0:T(8,128)(2,1)}, u32[]{:S(2)}, u32[]{:S(2)}) collective-permute-start(bf16[384,768]{1,0:T(8,128)(2,1)S(1)} %collective-permute-done.3.ya1), channel_id=1, source_target_pairs={{0,32},{32,0},{1,33},{33,1},{2,34},{34,2},{3,35},{35,3},{4,36},{36... | collective-permute-start | bytes 1769480 | tf_op jit(solution)/shard_map/ppermute | solution.py:361
  87.3 27.5 %shard_map.121 = (bf16[256,1536]{1,0:T(8,128)(2,1)}, bf16[256,1536]{1,0:T(8,128)(2,1)}, f32[512,128]{1,0:T(8,128)S(1)}) custom-call(s32[8]{0:T(128)S(1)} %stack.25.sc, bf16[256,1536]{1,0:T(8,128)(2,1)} %bitcast.24, bf16[256,1536]{1,0:T(8,128)(2,1)} %bitcast.26, bf16[96,1536]{1,0:T(8,128)(2,1)S(1)} %collective-permute-done.1.rim_a, ...), custom_call_target="tpu_custom_call" | custom-call | flops 8999999488 | bytes 14000000 | tf_op jit(solution)/shard_map/pallas_call | solution.py:251
  114.8 13.6 %all_to_all.20 = f32[32,16,128]{2,1,0:T(8,128)S(1)} all-to-all(f32[32,16,128]{2,1,0:T(8,128)S(1)} %bitcast.33), channel_id=1, replica_groups=mesh['zh'=2,'x'=4,'core'=2,'y'=4,'zl'=8] {'x','core','y'}, dimensions={0} | all-to-all | bytes 524288 | tf_op jit(solution)/shard_map/all_to_all | solution.py:367
  128.5 18.4 %all_to_all.21 = f32[16,16,128]{2,1,0:T(8,128)S(1)} all-to-all(f32[16,16,128]{2,1,0:T(8,128)S(1)} %broadcast_in_dim.20), channel_id=1, replica_groups=mesh['zh'=2,'x'=4,'core'=2,'y'=4,'zl'=8] {'zh','zl'}, dimensions={0} | all-to-all | bytes 262144 | tf_op jit(solution)/shard_map/all_to_all | solution.py:369
  146.9 15.4 %all_to_all.22 = f32[32,16,128]{2,1,0:T(8,128)S(1)} all-to-all(f32[32,16,128]{2,1,0:T(8,128)S(1)} %broadcast_in_dim.21), channel_id=1, replica_groups=mesh['zh'=2,'x'=4,'core'=2,'y'=4,'zl'=8] {'x','core','y'}, dimensions={0} | all-to-all | bytes 524288 | tf_op jit(solution)/shard_map/all_to_all | solution.py:371
  (30 shorter events, 5.4 us)
Async XLA Ops:
  7.2 80.2 %all-gather.2.cloned.1.call-start = ((), (), s32[]{:S(2)}) async-start(), calls=%async_computation.4 | async-start | bytes 5308416 | tf_op jit(solution)/shard_map/all_gather | solution.py:346
  8.9 25.3 %collective-permute-start = (bf16[96,768]{1,0:T(8,128)(2,1)S(1)}, bf16[96,768]{1,0:T(8,128)(2,1)S(1)}, u32[]{:S(2)}, u32[]{:S(2)}) collective-permute-start(bf16[96,768]{1,0:T(8,128)(2,1)S(1)} %constant_dynamic-slice_fusion), channel_id=1, source_target_pairs={{0,263},{1,262},{2,261},{3,260},{4,259},{5,258},{6,257},{7,256},{2... | collective-permute-start | bytes 442376 | tf_op jit(solution)/shard_map/ppermute | solution.py:347
  23.6 1.1 copy-start
  24.8 1.1 copy-start.1
  35.0 25.7 %all-to-all-start = ((bf16[4,96,768]{2,1,0:T(8,128)(2,1)}), bf16[4,96,768]{2,1,0:T(8,128)(2,1)S(1)}, u32[]{:S(2)}, u32[]{:S(2)}) async-start(bf16[4,96,768]{2,1,0:T(8,128)(2,1)} %shard_map.119), calls=%async_computation | async-start | bytes 1179648 | tf_op jit(solution)/shard_map/all_to_all | solution.py:352
  39.0 10.9 %collective-permute-start.1 = (bf16[96,1536]{1,0:T(8,128)(2,1)S(1)}, bf16[96,1536]{1,0:T(8,128)(2,1)S(1)}, u32[]{:S(2)}, u32[]{:S(2)}) collective-permute-start(bf16[96,1536]{1,0:T(8,128)(2,1)S(1)} %get-tuple-element.20), channel_id=1, source_target_pairs={{0,1},{1,0},{2,3},{3,2},{4,5},{5,4},{6,7},{7,6},{8,9},{9,8},{10,11... | collective-permute-start | bytes 884744 | tf_op jit(solution)/shard_map/ppermute | solution.py:350
  41.0 19.7 %collective-permute-start.2 = (bf16[96,1536]{1,0:T(8,128)(2,1)S(1)}, bf16[96,1536]{1,0:T(8,128)(2,1)S(1)}, u32[]{:S(2)}, u32[]{:S(2)}) collective-permute-start(bf16[96,1536]{1,0:T(8,128)(2,1)S(1)} %get-tuple-element.21), channel_id=1, source_target_pairs={{1,2},{2,1},{3,4},{4,3},{5,6},{6,5},{7,8},{8,7},{9,10},{10,9},{11,... | collective-permute-start | bytes 884744 | tf_op jit(solution)/shard_map/ppermute | solution.py:351
  60.7 15.1 %collective-permute-start.5 = (bf16[384,768]{1,0:T(8,128)(2,1)S(1)}, bf16[384,768]{1,0:T(8,128)(2,1)S(1)}, u32[]{:S(2)}, u32[]{:S(2)}) collective-permute-start(bf16[384,768]{1,0:T(8,128)(2,1)S(1)} %bitcast.28), channel_id=1, source_target_pairs={{0,24},{8,0},{16,8},{24,16},{1,25},{9,1},{17,9},{25,17},{2,26},{10... | collective-permute-start | bytes 1769480 | tf_op jit(solution)/shard_map/ppermute | solution.py:359
  62.8 17.5 %collective-permute-start.4 = (bf16[384,768]{1,0:T(8,128)(2,1)S(1)}, bf16[384,768]{1,0:T(8,128)(2,1)S(1)}, u32[]{:S(2)}, u32[]{:S(2)}) collective-permute-start(bf16[384,768]{1,0:T(8,128)(2,1)S(1)} %bitcast.29), channel_id=1, source_target_pairs={{0,1},{1,0},{2,3},{3,2},{4,5},{5,4},{6,7},{7,6},{8,9},{9,8},{10,11... | collective-permute-start | bytes 1769480 | tf_op jit(solution)/shard_map/ppermute | solution.py:358
  64.7 17.6 %collective-permute-start.3 = (bf16[384,768]{1,0:T(8,128)(2,1)S(1)}, bf16[384,768]{1,0:T(8,128)(2,1)S(1)}, u32[]{:S(2)}, u32[]{:S(2)}) collective-permute-start(bf16[384,768]{1,0:T(8,128)(2,1)S(1)} %bitcast.30), channel_id=1, source_target_pairs={{0,8},{8,16},{16,24},{24,0},{1,9},{9,17},{17,25},{25,1},{2,10},{10... | collective-permute-start | bytes 1769480 | tf_op jit(solution)/shard_map/ppermute | solution.py:357
  67.9 17.5 %collective-permute-start.6 = (bf16[384,768]{1,0:T(8,128)(2,1)S(1)}, bf16[384,768]{1,0:T(8,128)(2,1)S(1)}, u32[]{:S(2)}, u32[]{:S(2)}) collective-permute-start(bf16[384,768]{1,0:T(8,128)(2,1)S(1)} %bitcast.31), channel_id=1, source_target_pairs={{0,32},{32,0},{1,33},{33,1},{2,34},{34,2},{3,35},{35,3},{4,36},{36... | collective-permute-start | bytes 1769480 | tf_op jit(solution)/shard_map/ppermute | solution.py:361
  75.8 11.6 %copy-start.2 = (bf16[384,768]{1,0:T(8,128)(2,1)}, bf16[384,768]{1,0:T(8,128)(2,1)S(1)}, u32[]{:S(2)}) copy-start(bf16[384,768]{1,0:T(8,128)(2,1)S(1)} %collective-permute-done.5.ya3) | copy-start | bytes 1769476
  75.8 9.7 %collective-permute-start.9 = (bf16[384,768]{1,0:T(8,128)(2,1)S(1)}, bf16[384,768]{1,0:T(8,128)(2,1)S(1)}, u32[]{:S(2)}, u32[]{:S(2)}) collective-permute-start(bf16[384,768]{1,0:T(8,128)(2,1)S(1)} %collective-permute-done.5.ya3), channel_id=1, source_target_pairs={{0,32},{32,0},{1,33},{33,1},{2,34},{34,2},{3,35},{35,3},{4,36},{36... | collective-permute-start | bytes 1769480 | tf_op jit(solution)/shard_map/ppermute | solution.py:361
  80.3 5.3 %collective-permute-start.8 = (bf16[384,768]{1,0:T(8,128)(2,1)S(1)}, bf16[384,768]{1,0:T(8,128)(2,1)S(1)}, u32[]{:S(2)}, u32[]{:S(2)}) collective-permute-start(bf16[384,768]{1,0:T(8,128)(2,1)S(1)} %collective-permute-done.4.ya2), channel_id=1, source_target_pairs={{0,32},{32,0},{1,33},{33,1},{2,34},{34,2},{3,35},{35,3},{4,36},{36... | collective-permute-start | bytes 1769480 | tf_op jit(solution)/shard_map/ppermute | solution.py:361
  82.3 5.0 %collective-permute-start.7 = (bf16[384,768]{1,0:T(8,128)(2,1)S(1)}, bf16[384,768]{1,0:T(8,128)(2,1)}, u32[]{:S(2)}, u32[]{:S(2)}) collective-permute-start(bf16[384,768]{1,0:T(8,128)(2,1)S(1)} %collective-permute-done.3.ya1), channel_id=1, source_target_pairs={{0,32},{32,0},{1,33},{33,1},{2,34},{34,2},{3,35},{35,3},{4,36},{36... | collective-permute-start | bytes 1769480 | tf_op jit(solution)/shard_map/ppermute | solution.py:361
  85.5 0.8 copy-start.3
  85.5 1.0 copy-start.4
  86.5 0.8 copy-start.5
Sparse Core Ops, SparseCore 0:
  10.1 53.9 all-gather.1

commit v5 on v4

--- a/solution.py
+++ b/solution.py
@@ -34,8 +34,8 @@
 
 
 def fused(sc, x_hbm, og_hbm, rim_a, rim_b, dw, near, ya0, ya1, ya2, ya3, yb0, yb1, yb2, yb3,
-          act_ref, ig_ref, red_ref,
-          xe, oge, w, nrm, std, inv, gbuf, abuf, sbuf, slp, kacc, gh, gn,
+          act_hbm, ig_ref, red_ref,
+          act_ref, xe, oge, w, nrm, std, inv, gbuf, abuf, sbuf, slp, kacc, gh, gn,
           xsem, wsem):
     pos, length = sc[0], sc[1]
     zh, ci, turn = sc[2], sc[3], sc[4]
@@ -217,6 +217,8 @@
 
     lax.fori_loop(0, D // 256, chan_step, 0)
 
+    act_copy = pltpu.make_async_copy(act_ref, act_hbm, xsem.at[12])
+    act_copy.start()
     gn[...] = lax.dot_general(gh[...], w[...], (((1,), (1,)), ((), ())), preferred_element_type=F32)
 
     def grad_step(i, carry):
@@ -243,6 +245,7 @@
     for l in range(LT):
         red_ref[GAIN_ROW + l:GAIN_ROW + l + 1, :] = grow[:, l * 128:(l + 1) * 128]
         red_ref[BIAS_ROW + l:BIAS_ROW + l + 1, :] = brow[:, l * 128:(l + 1) * 128]
+    act_copy.wait()
 
 
 def run_fused(scalars, frames, out_grad, rim_a, rim_b, params, pieces):
@@ -256,8 +259,9 @@
             jax.ShapeDtypeStruct((PACK, 128), F32),
         ),
         in_specs=[pl.BlockSpec(memory_space=pltpu.SMEM)] + [any_spec] * 4 + [vm] + [any_spec] * len(pieces),
-        out_specs=(vm, vm, vm),
+        out_specs=(any_spec, vm, vm),
         scratch_shapes=[
+            pltpu.VMEM((2 * BLK, D), BF16),
             pltpu.VMEM((2 * EXT, D), BF16),
             pltpu.VMEM((2 * EXG, D), BF16),
             pltpu.VMEM((D, 2 * D), BF16),
@@ -271,7 +275,7 @@
             pltpu.VMEM((TAPS, 8, 128), F32),
             pltpu.VMEM((2 * BLK, 2 * D), BF16),
             pltpu.VMEM((2 * BLK, D), F32),
-            pltpu.SemaphoreType.DMA((12,)),
+            pltpu.SemaphoreType.DMA((13,)),
             pltpu.SemaphoreType.DMA((40,)),
         ],
         compiler_params=pltpu.CompilerParams(vmem_limit_bytes=51 * 1024 * 1024),

time: 171 us -> 171 us (level)
  no operation moved by 1% of the time
where the time goes in v5:
time: 171 us; the launch traced here: 170 us
  starting transfers between devices  47.8 us (28%)
  blocking collectives  47.4 us (28%)
  Pallas kernels  29.7 us (17%)
  waiting for transfers between devices  21.1 us (12%)
  between operations  15.6 us (9%)
  local copies, waits for them, and re-layouts  7.83 us (5%)
    pallas_call x1, Pallas kernels, run_fused(): pl.pallas_call(fused, out_shape=(jax.ShapeDtypeStruct((2 * BLK, D), BF16)...  27.5 us
    all_to_all x1, blocking collectives, reduce_all(): lax.all_to_all(jnp.broadcast_to(mine[None], (16,) + mine.shape), ('zh', '...  18.4 us
    all_to_all x1, blocking collectives, reduce_all(): lax.all_to_all(jnp.broadcast_to(mine[None], (32,) + mine.shape), plane, 0...  15.4 us
    ppermute x4, starting transfers between devices, gather_weight(): yb = [lax.ppermute(part, 'core', shift(2, 1)) for part in ya]  13.8 us
    all_to_all x1, blocking collectives, reduce_all(): parts = lax.all_to_all(packed.reshape(32, PACK // 32, 128), plane, 0, 0)  13.6 us
    ppermute x1, starting transfers between devices, gather_weight(): far = lax.ppermute(quarter, ('zh', 'zl'), [(i, 15 - i) for i in range(16)])  12 us
    ppermute x1, waiting for transfers between devices, gather_weight(): b = lax.ppermute(rim_b, ('y', 'zl'), meet_next())  10.8 us
    ppermute x1, starting transfers between devices, gather_weight(): b = lax.ppermute(rim_b, ('y', 'zl'), meet_next())  8.94 us
  transfers between devices with their start and end apart: 12, of which 3 were waited for; matrix products, arithmetic and copies ran while one was open for 2% of the time, Pallas kernels for 1%

profile of v5, /device:TPU:1, one launch (start us, length us, event | category | flops | bytes accessed | tf_op | source)
XLA Modules:
  0.0 170.5 jit_solution(1625190100043962135)
XLA Ops:
  7.9 0.9 constant_dynamic-slice_fusion
  8.9 12.0 %collective-permute-start = (bf16[96,768]{1,0:T(8,128)(2,1)S(1)}, bf16[96,768]{1,0:T(8,128)(2,1)S(1)}, u32[]{:S(2)}, u32[]{:S(2)}) collective-permute-start(bf16[96,768]{1,0:T(8,128)(2,1)S(1)} %constant_dynamic-slice_fusion), channel_id=1, source_target_pairs={{0,263},{1,262},{2,261},{3,260},{4,259},{5,258},{6,257},{7,256},{2... | collective-permute-start | bytes 442376 | tf_op jit(solution)/shard_map/ppermute | solution.py:351
  23.6 1.1 copy-done
  24.8 1.1 copy-done.1
  25.9 1.4 shard_map.120
  27.3 1.0 pad_maximum_fusion.dw
  28.3 5.9 %collective-permute-done.src = bf16[96,768]{1,0:T(8,128)(2,1)S(1)} collective-permute-done((bf16[96,768]{1,0:T(8,128)(2,1)S(1)}, bf16[96,768]{1,0:T(8,128)(2,1)S(1)}, u32[]{:S(2)}, u32[]{:S(2)}) %collective-permute-start) | collective-permute-done | bytes 147488 | tf_op jit(solution)/shard_map/ppermute | solution.py:351
  34.2 0.8 shard_map.119
  35.0 4.0 %all-to-all-start = ((bf16[4,96,768]{2,1,0:T(8,128)(2,1)}), bf16[4,96,768]{2,1,0:T(8,128)(2,1)S(1)}, u32[]{:S(2)}, u32[]{:S(2)}) async-start(bf16[4,96,768]{2,1,0:T(8,128)(2,1)} %shard_map.119), calls=%async_computation | async-start | bytes 1179648 | tf_op jit(solution)/shard_map/all_to_all | solution.py:356
  39.0 1.9 %collective-permute-start.1 = (bf16[96,1536]{1,0:T(8,128)(2,1)S(1)}, bf16[96,1536]{1,0:T(8,128)(2,1)S(1)}, u32[]{:S(2)}, u32[]{:S(2)}) collective-permute-start(bf16[96,1536]{1,0:T(8,128)(2,1)S(1)} %get-tuple-element.20), channel_id=1, source_target_pairs={{0,1},{1,0},{2,3},{3,2},{4,5},{5,4},{6,7},{7,6},{8,9},{9,8},{10,11... | collective-permute-start | bytes 884744 | tf_op jit(solution)/shard_map/ppermute | solution.py:354
  41.0 8.9 %collective-permute-start.2 = (bf16[96,1536]{1,0:T(8,128)(2,1)S(1)}, bf16[96,1536]{1,0:T(8,128)(2,1)S(1)}, u32[]{:S(2)}, u32[]{:S(2)}) collective-permute-start(bf16[96,1536]{1,0:T(8,128)(2,1)S(1)} %get-tuple-element.21), channel_id=1, source_target_pairs={{1,2},{2,1},{3,4},{4,3},{5,6},{6,5},{7,8},{8,7},{9,10},{10,9},{11,... | collective-permute-start | bytes 884744 | tf_op jit(solution)/shard_map/ppermute | solution.py:355
  49.9 10.8 %collective-permute-done.2.rim_b = bf16[96,1536]{1,0:T(8,128)(2,1)S(1)} collective-permute-done((bf16[96,1536]{1,0:T(8,128)(2,1)S(1)}, bf16[96,1536]{1,0:T(8,128)(2,1)S(1)}, u32[]{:S(2)}, u32[]{:S(2)}) %collective-permute-start.2) | collective-permute-done | bytes 294944 | tf_op jit(solution)/shard_map/ppermute | solution.py:355
  60.7 2.1 %collective-permute-start.5 = (bf16[384,768]{1,0:T(8,128)(2,1)S(1)}, bf16[384,768]{1,0:T(8,128)(2,1)S(1)}, u32[]{:S(2)}, u32[]{:S(2)}) collective-permute-start(bf16[384,768]{1,0:T(8,128)(2,1)S(1)} %bitcast.28), channel_id=1, source_target_pairs={{0,24},{8,0},{16,8},{24,16},{1,25},{9,1},{17,9},{25,17},{2,26},{10... | collective-permute-start | bytes 1769480 | tf_op jit(solution)/shard_map/ppermute | solution.py:363
  62.8 1.9 %collective-permute-start.4 = (bf16[384,768]{1,0:T(8,128)(2,1)S(1)}, bf16[384,768]{1,0:T(8,128)(2,1)S(1)}, u32[]{:S(2)}, u32[]{:S(2)}) collective-permute-start(bf16[384,768]{1,0:T(8,128)(2,1)S(1)} %bitcast.29), channel_id=1, source_target_pairs={{0,1},{1,0},{2,3},{3,2},{4,5},{5,4},{6,7},{7,6},{8,9},{9,8},{10,11... | collective-permute-start | bytes 1769480 | tf_op jit(solution)/shard_map/ppermute | solution.py:362
  64.7 3.2 %collective-permute-start.3 = (bf16[384,768]{1,0:T(8,128)(2,1)S(1)}, bf16[384,768]{1,0:T(8,128)(2,1)S(1)}, u32[]{:S(2)}, u32[]{:S(2)}) collective-permute-start(bf16[384,768]{1,0:T(8,128)(2,1)S(1)} %bitcast.30), channel_id=1, source_target_pairs={{0,8},{8,16},{16,24},{24,0},{1,9},{9,17},{17,25},{25,1},{2,10},{10... | collective-permute-start | bytes 1769480 | tf_op jit(solution)/shard_map/ppermute | solution.py:361
  67.9 4.1 %collective-permute-start.6 = (bf16[384,768]{1,0:T(8,128)(2,1)S(1)}, bf16[384,768]{1,0:T(8,128)(2,1)S(1)}, u32[]{:S(2)}, u32[]{:S(2)}) collective-permute-start(bf16[384,768]{1,0:T(8,128)(2,1)S(1)} %bitcast.31), channel_id=1, source_target_pairs={{0,32},{32,0},{1,33},{33,1},{2,34},{34,2},{3,35},{35,3},{4,36},{36... | collective-permute-start | bytes 1769480 | tf_op jit(solution)/shard_map/ppermute | solution.py:365
  72.0 3.7 %collective-permute-done.5.ya3 = bf16[384,768]{1,0:T(8,128)(2,1)S(1)} collective-permute-done((bf16[384,768]{1,0:T(8,128)(2,1)S(1)}, bf16[384,768]{1,0:T(8,128)(2,1)S(1)}, u32[]{:S(2)}, u32[]{:S(2)}) %collective-permute-start.5) | collective-permute-done | bytes 589856 | tf_op jit(solution)/shard_map/ppermute | solution.py:363
  75.8 4.5 %collective-permute-start.9 = (bf16[384,768]{1,0:T(8,128)(2,1)S(1)}, bf16[384,768]{1,0:T(8,128)(2,1)S(1)}, u32[]{:S(2)}, u32[]{:S(2)}) collective-permute-start(bf16[384,768]{1,0:T(8,128)(2,1)S(1)} %collective-permute-done.5.ya3), channel_id=1, source_target_pairs={{0,32},{32,0},{1,33},{33,1},{2,34},{34,2},{3,35},{35,3},{4,36},{36... | collective-permute-start | bytes 1769480 | tf_op jit(solution)/shard_map/ppermute | solution.py:365
  80.3 2.1 %collective-permute-start.8 = (bf16[384,768]{1,0:T(8,128)(2,1)S(1)}, bf16[384,768]{1,0:T(8,128)(2,1)S(1)}, u32[]{:S(2)}, u32[]{:S(2)}) collective-permute-start(bf16[384,768]{1,0:T(8,128)(2,1)S(1)} %collective-permute-done.4.ya2), channel_id=1, source_target_pairs={{0,32},{32,0},{1,33},{33,1},{2,34},{34,2},{3,35},{35,3},{4,36},{36... | collective-permute-start | bytes 1769480 | tf_op jit(solution)/shard_map/ppermute | solution.py:365
  82.3 3.1 %collective-permute-start.7 = (bf16[384,768]{1,0:T(8,128)(2,1)S(1)}, bf16[384,768]{1,0:T(8,128)(2,1)}, u32[]{:S(2)}, u32[]{:S(2)}) collective-permute-start(bf16[384,768]{1,0:T(8,128)(2,1)S(1)} %collective-permute-done.3.ya1), channel_id=1, source_target_pairs={{0,32},{32,0},{1,33},{33,1},{2,34},{34,2},{3,35},{35,3},{4,36},{36... | collective-permute-start | bytes 1769480 | tf_op jit(solution)/shard_map/ppermute | solution.py:365
  87.3 27.5 %shard_map.121 = (bf16[256,1536]{1,0:T(8,128)(2,1)}, bf16[256,1536]{1,0:T(8,128)(2,1)}, f32[512,128]{1,0:T(8,128)S(1)}) custom-call(s32[8]{0:T(128)S(1)} %stack.25.sc, bf16[256,1536]{1,0:T(8,128)(2,1)} %bitcast.24, bf16[256,1536]{1,0:T(8,128)(2,1)} %bitcast.26, bf16[96,1536]{1,0:T(8,128)(2,1)S(1)} %collective-permute-done.1.rim_a, ...), custom_call_target="tpu_custom_call" | custom-call | flops 8999999488 | bytes 14000000 | tf_op jit(solution)/shard_map/pallas_call | solution.py:254
  114.8 13.6 %all_to_all.20 = f32[32,16,128]{2,1,0:T(8,128)S(1)} all-to-all(f32[32,16,128]{2,1,0:T(8,128)S(1)} %bitcast.33), channel_id=1, replica_groups=mesh['zh'=2,'x'=4,'core'=2,'y'=4,'zl'=8] {'x','core','y'}, dimensions={0} | all-to-all | bytes 524288 | tf_op jit(solution)/shard_map/all_to_all | solution.py:371
  128.5 18.4 %all_to_all.21 = f32[16,16,128]{2,1,0:T(8,128)S(1)} all-to-all(f32[16,16,128]{2,1,0:T(8,128)S(1)} %broadcast_in_dim.20), channel_id=1, replica_groups=mesh['zh'=2,'x'=4,'core'=2,'y'=4,'zl'=8] {'zh','zl'}, dimensions={0} | all-to-all | bytes 262144 | tf_op jit(solution)/shard_map/all_to_all | solution.py:373
  147.0 15.4 %all_to_all.22 = f32[32,16,128]{2,1,0:T(8,128)S(1)} all-to-all(f32[32,16,128]{2,1,0:T(8,128)S(1)} %broadcast_in_dim.21), channel_id=1, replica_groups=mesh['zh'=2,'x'=4,'core'=2,'y'=4,'zl'=8] {'x','core','y'}, dimensions={0} | all-to-all | bytes 524288 | tf_op jit(solution)/shard_map/all_to_all | solution.py:375
  (30 shorter events, 5.4 us)
Async XLA Ops:
  7.2 80.2 %all-gather.2.cloned.1.call-start = ((), (), s32[]{:S(2)}) async-start(), calls=%async_computation.4 | async-start | bytes 5308416 | tf_op jit(solution)/shard_map/all_gather | solution.py:350
  8.9 25.3 %collective-permute-start = (bf16[96,768]{1,0:T(8,128)(2,1)S(1)}, bf16[96,768]{1,0:T(8,128)(2,1)S(1)}, u32[]{:S(2)}, u32[]{:S(2)}) collective-permute-start(bf16[96,768]{1,0:T(8,128)(2,1)S(1)} %constant_dynamic-slice_fusion), channel_id=1, source_target_pairs={{0,263},{1,262},{2,261},{3,260},{4,259},{5,258},{6,257},{7,256},{2... | collective-permute-start | bytes 442376 | tf_op jit(solution)/shard_map/ppermute | solution.py:351
  23.6 1.1 copy-start
  24.8 1.1 copy-start.1
  35.0 25.7 %all-to-all-start = ((bf16[4,96,768]{2,1,0:T(8,128)(2,1)}), bf16[4,96,768]{2,1,0:T(8,128)(2,1)S(1)}, u32[]{:S(2)}, u32[]{:S(2)}) async-start(bf16[4,96,768]{2,1,0:T(8,128)(2,1)} %shard_map.119), calls=%async_computation | async-start | bytes 1179648 | tf_op jit(solution)/shard_map/all_to_all | solution.py:356
  39.0 10.9 %collective-permute-start.1 = (bf16[96,1536]{1,0:T(8,128)(2,1)S(1)}, bf16[96,1536]{1,0:T(8,128)(2,1)S(1)}, u32[]{:S(2)}, u32[]{:S(2)}) collective-permute-start(bf16[96,1536]{1,0:T(8,128)(2,1)S(1)} %get-tuple-element.20), channel_id=1, source_target_pairs={{0,1},{1,0},{2,3},{3,2},{4,5},{5,4},{6,7},{7,6},{8,9},{9,8},{10,11... | collective-permute-start | bytes 884744 | tf_op jit(solution)/shard_map/ppermute | solution.py:354
  41.0 19.7 %collective-permute-start.2 = (bf16[96,1536]{1,0:T(8,128)(2,1)S(1)}, bf16[96,1536]{1,0:T(8,128)(2,1)S(1)}, u32[]{:S(2)}, u32[]{:S(2)}) collective-permute-start(bf16[96,1536]{1,0:T(8,128)(2,1)S(1)} %get-tuple-element.21), channel_id=1, source_target_pairs={{1,2},{2,1},{3,4},{4,3},{5,6},{6,5},{7,8},{8,7},{9,10},{10,9},{11,... | collective-permute-start | bytes 884744 | tf_op jit(solution)/shard_map/ppermute | solution.py:355
  60.7 15.1 %collective-permute-start.5 = (bf16[384,768]{1,0:T(8,128)(2,1)S(1)}, bf16[384,768]{1,0:T(8,128)(2,1)S(1)}, u32[]{:S(2)}, u32[]{:S(2)}) collective-permute-start(bf16[384,768]{1,0:T(8,128)(2,1)S(1)} %bitcast.28), channel_id=1, source_target_pairs={{0,24},{8,0},{16,8},{24,16},{1,25},{9,1},{17,9},{25,17},{2,26},{10... | collective-permute-start | bytes 1769480 | tf_op jit(solution)/shard_map/ppermute | solution.py:363
  62.8 17.5 %collective-permute-start.4 = (bf16[384,768]{1,0:T(8,128)(2,1)S(1)}, bf16[384,768]{1,0:T(8,128)(2,1)S(1)}, u32[]{:S(2)}, u32[]{:S(2)}) collective-permute-start(bf16[384,768]{1,0:T(8,128)(2,1)S(1)} %bitcast.29), channel_id=1, source_target_pairs={{0,1},{1,0},{2,3},{3,2},{4,5},{5,4},{6,7},{7,6},{8,9},{9,8},{10,11... | collective-permute-start | bytes 1769480 | tf_op jit(solution)/shard_map/ppermute | solution.py:362
  64.7 17.6 %collective-permute-start.3 = (bf16[384,768]{1,0:T(8,128)(2,1)S(1)}, bf16[384,768]{1,0:T(8,128)(2,1)S(1)}, u32[]{:S(2)}, u32[]{:S(2)}) collective-permute-start(bf16[384,768]{1,0:T(8,128)(2,1)S(1)} %bitcast.30), channel_id=1, source_target_pairs={{0,8},{8,16},{16,24},{24,0},{1,9},{9,17},{17,25},{25,1},{2,10},{10... | collective-permute-start | bytes 1769480 | tf_op jit(solution)/shard_map/ppermute | solution.py:361
  67.9 17.5 %collective-permute-start.6 = (bf16[384,768]{1,0:T(8,128)(2,1)S(1)}, bf16[384,768]{1,0:T(8,128)(2,1)S(1)}, u32[]{:S(2)}, u32[]{:S(2)}) collective-permute-start(bf16[384,768]{1,0:T(8,128)(2,1)S(1)} %bitcast.31), channel_id=1, source_target_pairs={{0,32},{32,0},{1,33},{33,1},{2,34},{34,2},{3,35},{35,3},{4,36},{36... | collective-permute-start | bytes 1769480 | tf_op jit(solution)/shard_map/ppermute | solution.py:365
  75.8 11.6 %copy-start.2 = (bf16[384,768]{1,0:T(8,128)(2,1)}, bf16[384,768]{1,0:T(8,128)(2,1)S(1)}, u32[]{:S(2)}) copy-start(bf16[384,768]{1,0:T(8,128)(2,1)S(1)} %collective-permute-done.5.ya3) | copy-start | bytes 1769476
  75.8 9.7 %collective-permute-start.9 = (bf16[384,768]{1,0:T(8,128)(2,1)S(1)}, bf16[384,768]{1,0:T(8,128)(2,1)S(1)}, u32[]{:S(2)}, u32[]{:S(2)}) collective-permute-start(bf16[384,768]{1,0:T(8,128)(2,1)S(1)} %collective-permute-done.5.ya3), channel_id=1, source_target_pairs={{0,32},{32,0},{1,33},{33,1},{2,34},{34,2},{3,35},{35,3},{4,36},{36... | collective-permute-start | bytes 1769480 | tf_op jit(solution)/shard_map/ppermute | solution.py:365
  80.3 5.3 %collective-permute-start.8 = (bf16[384,768]{1,0:T(8,128)(2,1)S(1)}, bf16[384,768]{1,0:T(8,128)(2,1)S(1)}, u32[]{:S(2)}, u32[]{:S(2)}) collective-permute-start(bf16[384,768]{1,0:T(8,128)(2,1)S(1)} %collective-permute-done.4.ya2), channel_id=1, source_target_pairs={{0,32},{32,0},{1,33},{33,1},{2,34},{34,2},{3,35},{35,3},{4,36},{36... | collective-permute-start | bytes 1769480 | tf_op jit(solution)/shard_map/ppermute | solution.py:365
  82.3 5.0 %collective-permute-start.7 = (bf16[384,768]{1,0:T(8,128)(2,1)S(1)}, bf16[384,768]{1,0:T(8,128)(2,1)}, u32[]{:S(2)}, u32[]{:S(2)}) collective-permute-start(bf16[384,768]{1,0:T(8,128)(2,1)S(1)} %collective-permute-done.3.ya1), channel_id=1, source_target_pairs={{0,32},{32,0},{1,33},{33,1},{2,34},{34,2},{3,35},{35,3},{4,36},{36... | collective-permute-start | bytes 1769480 | tf_op jit(solution)/shard_map/ppermute | solution.py:365
  85.5 0.8 copy-start.3
  85.5 1.0 copy-start.4
  86.5 0.8 copy-start.5
Sparse Core Ops, SparseCore 0:
  10.1 53.9 all-gather.1
